TPU v7x, 256 devices: a whole 4x4x8 slice. The times are simulated.
256 devices in a mesh: src: 16 (over y_hi, x, core), tgt: 16 (over z, y_lo).
Axes of the slice: x: 4, y: 4 (y_hi: 2, y_lo: 2; y = y_hi * 2 + y_lo), z: 8, core: 2. Of those that a mesh axis runs over, the one named last changes fastest.
Arguments:
- source_cells: bfloat16 [32, 524288], P(None, 'src'), may hold values from -4 to 4
- target_cells: bfloat16 [32, 524288], P(None, 'tgt'), may hold values from -4 to 4
- source_mass: float32 [524288], P('src'), may hold values from 0.5 to 2
- target_mass: float32 [524288], P('tgt'), may hold values from 0.5 to 2
- source_count: int32 [2048], P('src'), may hold values from 1 to 256, 393216 in all
- target_count: int32 [2048], P('tgt'), may hold values from 1 to 256, 393216 in all
- pair_lists: int32 [2048, 8], P('src'), may hold values from 0 to 2047, as said below
Outputs:
- source_potential: float32 [524288], P('src')
- target_potential: float32 [524288], P('tgt')
- mapped: float32 [32, 524288], P(None, ('src', 'tgt'))
Inputs may be any that keep to these rules, and one draw needn't show every extreme that they name: `pair_lists`: each row names 8 different target clusters, and every target cluster is named by some row. Within the rows of one index of src, the target clusters of one index of tgt are named 128 times in all, those of the next index of tgt (wrapping around) never, and those of every other index of tgt 128 // 2 times.
All inputs are finite; a program needn't handle non-finite values. No bound on the sum of `source_count` or of `target_count` on one device may be relied on, other than what follows from the above.
Results may differ from a plain program's by a relative error of at most 0.0003.
Values may be sent and summed in bfloat16 or wider, within the bound.
A program may use at most 64 MiB of HBM per device.

v0:
```python
import jax
import jax.numpy as jnp
from jax import lax
from jax.sharding import PartitionSpec as P

ITERS = 2


entropy_blur = 0.5
empty_peak = -1e30


def squared_norms(cells):
    widened = cells.astype(jnp.float32)
    return jnp.sum(widened * widened, axis=0)


def potential(logmass, usable, highest, totals):
    safe_totals = jnp.where(usable, totals, 1.0)
    return jnp.where(
        usable, entropy_blur * logmass - entropy_blur * (highest + jnp.log(safe_totals)), 0.0
    )


def pair_table(pair_lists, tgt_block, per_block, capacity):
    list_width = pair_lists.shape[1]
    flat_ids = pair_lists.reshape(-1)
    chosen = flat_ids // per_block == tgt_block
    slot_rank = jnp.cumsum(chosen.astype(jnp.int32)) - 1
    slot_ids = jnp.arange(capacity, dtype=jnp.int32)
    matches = (slot_rank[None, :] == slot_ids[:, None]) & chosen[None, :]
    source_ids = jnp.arange(flat_ids.shape[0], dtype=jnp.int32) // list_width
    pair_src = jnp.sum(jnp.where(matches, source_ids[None, :], 0), axis=1)
    pair_tgt = jnp.sum(jnp.where(matches, (flat_ids % per_block)[None, :], 0), axis=1)
    is_live = jnp.any(matches, axis=1)
    return (pair_src, pair_tgt, is_live)


def fold_tiles(maxima, totals, cluster_of, is_live, clusters):
    member = (
        (cluster_of[None, :] == jnp.arange(clusters, dtype=jnp.int32)[:, None]) & is_live[None, :]
    ).astype(jnp.float32)
    maxima = jnp.where(is_live[:, None], maxima, empty_peak)
    totals = jnp.where(is_live[:, None], totals, 0.0)
    highest = jnp.max(jnp.where(member[:, :, None] > 0.5, maxima[None], empty_peak), axis=1)
    spread_max = jnp.dot(member.T, highest, precision=lax.Precision.HIGHEST)
    rescale = jnp.exp(maxima - spread_max)
    summed = jnp.dot(member, totals * rescale, precision=lax.Precision.HIGHEST)
    return (highest, summed, member, rescale)


def shards(
    source_cells, target_cells, source_mass, target_mass, source_count, target_count, pair_lists
):
    features = source_cells.shape[0]
    src_clusters = source_count.shape[0]
    tgt_clusters = target_count.shape[0]
    tile_cells = source_cells.shape[1] // src_clusters
    capacity = 2 * pair_lists.size // lax.axis_size("tgt")
    tgt_index = lax.axis_index("tgt")
    position = jnp.arange(tile_cells, dtype=jnp.int32)
    src_usable = position[None, :] < source_count[:, None]
    tgt_usable = position[None, :] < target_count[:, None]
    src_tiles = source_cells.reshape(features, src_clusters, tile_cells)
    tgt_tiles = target_cells.reshape(features, tgt_clusters, tile_cells)
    src_norm = squared_norms(source_cells).reshape(src_clusters, tile_cells)
    src_logmass = jnp.log(source_mass).reshape(src_clusters, tile_cells)
    tgt_logmass = jnp.log(target_mass).reshape(tgt_clusters, tile_cells)
    own_src, own_tgt, own_live = pair_table(pair_lists, tgt_index, tgt_clusters, capacity)
    own_cells = jnp.take(tgt_tiles, own_tgt, axis=1)
    own_usable = jnp.take(tgt_usable, own_tgt, axis=0)

    def target_side(target_pot):
        return jnp.take(target_pot, own_tgt, axis=0)

    work_src_cells = jnp.take(src_tiles, own_src, axis=1)
    work_src_norm = jnp.take(src_norm, own_src, axis=0)
    work_src_usable = jnp.take(src_usable, own_src, axis=0)
    work_tgt_norm = squared_norms(own_cells)
    tile_count = own_src.shape[0]
    group_size = 8
    group_count = tile_count // group_size

    def tile_sweep(sweep_kind, left_pot, right_pot):

        def one_group(group_index):
            offset = group_index * group_size

            def window(values, along):
                return lax.dynamic_slice_in_dim(values, offset, group_size, along)

            src_part = window(work_src_cells, 1)
            tgt_part = window(own_cells, 1)
            cross_term = jnp.einsum(
                "dpi,dpj->pij", src_part, tgt_part, preferred_element_type=jnp.float32
            )
            distance = (
                window(work_src_norm, 0)[:, :, None]
                + window(work_tgt_norm, 0)[:, None, :]
                - 2.0 * cross_term
            )
            if sweep_kind == "columns":
                usable = window(work_src_usable, 0)[:, :, None]
                scores = jnp.where(
                    usable, (window(left_pot, 0)[:, :, None] - distance) / entropy_blur, empty_peak
                )
                maxima = jnp.max(scores, axis=1)
                totals = jnp.sum(
                    jnp.where(usable, jnp.exp(scores - maxima[:, None, :]), 0.0), axis=1
                )
                return (maxima, totals)
            usable = window(own_usable, 0)[:, None, :]
            scores = jnp.where(
                usable, (window(right_pot, 0)[:, None, :] - distance) / entropy_blur, empty_peak
            )
            maxima = jnp.max(scores, axis=2)
            weight = jnp.where(usable, jnp.exp(scores - maxima[:, :, None]), 0.0)
            totals = jnp.sum(weight, axis=2)
            if sweep_kind == "rows":
                return (maxima, totals)
            carried = jnp.einsum(
                "pij,dpj->dpi",
                weight,
                tgt_part.astype(jnp.float32),
                precision=lax.Precision.HIGHEST,
            )
            return (maxima, totals, carried)

        results = lax.map(one_group, jnp.arange(group_count, dtype=jnp.int32))
        maxima = results[0].reshape(tile_count, tile_cells)
        totals = results[1].reshape(tile_count, tile_cells)
        if sweep_kind == "map":
            return (maxima, totals, results[2])
        return (maxima, totals)

    target_pot = jnp.zeros((tgt_clusters, tile_cells), jnp.float32)
    source_pot = jnp.zeros((src_clusters, tile_cells), jnp.float32)
    for sweep_index in range(ITERS):
        if sweep_index == 0:
            right_side = jnp.zeros((tile_count, tile_cells), jnp.float32)
        else:
            right_side = target_side(target_pot)
        maxima, totals = tile_sweep("rows", None, right_side)
        highest, summed, member, rescale = fold_tiles(
            maxima, totals, own_src, own_live, src_clusters
        )
        source_global_max = lax.pmax(highest, "tgt")
        highest, summed = (
            source_global_max,
            lax.psum(summed * jnp.exp(highest - source_global_max), "tgt"),
        )
        source_pot = potential(src_logmass, src_usable, highest, summed)
        left_side = jnp.take(source_pot, own_src, axis=0)
        maxima, totals = tile_sweep("columns", left_side, None)
        maxima, totals = (maxima, totals)
        highest, summed, member, rescale = fold_tiles(
            maxima, totals, own_tgt, own_live, tgt_clusters
        )
        target_global_max = lax.pmax(highest, "src")
        highest, summed = (
            target_global_max,
            lax.psum(summed * jnp.exp(highest - target_global_max), "src"),
        )
        target_pot = potential(tgt_logmass, tgt_usable, highest, summed)
    right_side = target_side(target_pot)
    maxima, totals, carried = tile_sweep("map", None, right_side)
    highest, summed, member, rescale = fold_tiles(maxima, totals, own_src, own_live, src_clusters)
    carried = carried * rescale.reshape(group_count, 1, group_size, tile_cells)
    gathered_rows = jnp.einsum(
        "puq,utqj->tpj",
        member.reshape(src_clusters, group_count, group_size),
        carried,
        precision=lax.Precision.HIGHEST,
    )
    global_max = lax.pmax(highest, "tgt")
    factor = jnp.exp(highest - global_max)
    numerator = (gathered_rows * factor[None]).reshape(features, src_clusters * tile_cells)
    denominator = (summed * factor).reshape(-1)
    live_rows = src_usable.reshape(-1)
    numerator, denominator = lax.psum((numerator, denominator), "tgt")
    share_rows = denominator.shape[0] // lax.axis_size("tgt")
    row_start = tgt_index * share_rows
    numerator = lax.dynamic_slice_in_dim(numerator, row_start, share_rows, 1)
    denominator = lax.dynamic_slice_in_dim(denominator, row_start, share_rows, 0)
    live_rows = lax.dynamic_slice_in_dim(live_rows, row_start, share_rows, 0)
    mapped = jnp.where(
        live_rows[None, :], numerator / jnp.where(live_rows, denominator, 1.0)[None, :], 0.0
    )
    return (source_pot.reshape(-1), target_pot.reshape(-1), mapped)


def solution(mesh):
    return jax.shard_map(
        shards,
        mesh=mesh,
        in_specs=(
            P(None, "src"),
            P(None, "tgt"),
            P("src"),
            P("tgt"),
            P("src"),
            P("tgt"),
            P("src", None),
        ),
        out_specs=(P("src"), P("tgt"), P(None, ("src", "tgt"))),
        check_vma=False,
    )
```

profile of v0, /device:TPU:24, one launch (start us, length us, event | category | flops | bytes accessed | tf_op | source)
XLA Modules:
  0.0 1915.5 jit_solution(6354788287100317251)
XLA Ops:
  9.4 2.2 multiply_reduce_fusion.1
  13.3 2.3 gather_fusion.4
  20.4 2.3 gather_fusion.3
  23.5 2.2 multiply_reduce_fusion
  25.8 61.7 %while.62 = (s32[]{:T(128)}, f32[16,8,256]{2,1,0:T(8,128)S(1)}, f32[16,8,256]{2,1,0:T(8,128)S(1)}, s32[16]{0:T(128)S(1)}, pred[128,256]{1,0:T(8,128)(4,1)S(1)}, ...) while((s32[]{:T(128)}, f32[16,8,256]{2,1,0:T(8,128)S(1)}, ...), condition=%wide.region_10.14_spmd, body=%wide.region_7.13_spmd.sunk | while | flops 38793220 | bytes 4572359 | solution.py:129
  87.7 5.3 select_reduce_fusion.8
  95.2 135.3 %all-reduce.12.cloned.1.call-done = f32[128,256]{1,0:T(8,128)} async-done(((f32[128,256]{1,0:T(8,128)}), f32[128,256]{1,0:T(8,128)}) %all-reduce.12.cloned.1.call-update) | async-done | bytes 131088 | tf_op jit(solution)/shard_map/pmax | solution.py:147
  232.6 136.2 %all-reduce.14.cloned.1.call-done = f32[128,256]{1,0:T(8,128)} async-done(((f32[128,256]{1,0:T(8,128)}), f32[128,256]{1,0:T(8,128)}) %all-reduce.14.cloned.1.call-update) | async-done | bytes 131088 | tf_op jit(solution)/shard_map/psum | solution.py:150
  370.8 63.9 %while.63 = (s32[]{:T(128)}, f32[16,8,256]{2,1,0:T(8,128)S(1)}, f32[16,8,256]{2,1,0:T(8,128)S(1)}, s32[16]{0:T(128)S(1)}, pred[128,256]{1,0:T(8,128)(4,1)S(1)}, ...) while((s32[]{:T(128)}, f32[16,8,256]{2,1,0:T(8,128)S(1)}, ...), condition=%wide.region_17.21_spmd, body=%wide.region_14.20_spmd.sunk | while | flops 38793220 | bytes 4596947 | solution.py:129
  376.1 2.1 fusion.116
  424.0 2.1 fusion.116
  428.0 2.1 fusion.116
  432.0 2.1 fusion.116
  434.7 5.3 select_reduce_fusion.7
  441.3 140.1 %all-reduce.16.cloned.1.call-done = f32[128,256]{1,0:T(8,128)} async-done(((f32[128,256]{1,0:T(8,128)}), f32[128,256]{1,0:T(8,128)}) %all-reduce.16.cloned.1.call-update) | async-done | bytes 131088 | tf_op jit(solution)/shard_map/pmax | solution.py:159
  583.4 143.9 %all-reduce.18.cloned.1.call-done = f32[128,256]{1,0:T(8,128)} async-done(((f32[128,256]{1,0:T(8,128)}), f32[128,256]{1,0:T(8,128)}) %all-reduce.18.cloned.1.call-update) | async-done | bytes 131088 | tf_op jit(solution)/shard_map/psum | solution.py:162
  729.2 63.9 %while.64 = (s32[]{:T(128)}, f32[16,8,256]{2,1,0:T(8,128)S(1)}, f32[16,8,256]{2,1,0:T(8,128)S(1)}, s32[16]{0:T(128)S(1)}, pred[128,256]{1,0:T(8,128)(4,1)S(1)}, ...) while((s32[]{:T(128)}, f32[16,8,256]{2,1,0:T(8,128)S(1)}, ...), condition=%wide.region_24.28_spmd, body=%wide.region_21.27_spmd.sunk | while | flops 38793220 | bytes 4596947 | solution.py:129
  782.4 2.1 fusion.117
  786.4 2.1 fusion.117
  790.4 2.1 fusion.117
  793.2 5.3 select_reduce_fusion.6
  799.8 135.1 %all-reduce.20.cloned.1.call-done = f32[128,256]{1,0:T(8,128)} async-done(((f32[128,256]{1,0:T(8,128)}), f32[128,256]{1,0:T(8,128)}) %all-reduce.20.cloned.1.call-update) | async-done | bytes 131088 | tf_op jit(solution)/shard_map/pmax | solution.py:147
  937.0 136.0 %all-reduce.22.cloned.1.call-done = f32[128,256]{1,0:T(8,128)} async-done(((f32[128,256]{1,0:T(8,128)}), f32[128,256]{1,0:T(8,128)}) %all-reduce.22.cloned.1.call-update) | async-done | bytes 131088 | tf_op jit(solution)/shard_map/psum | solution.py:150
  1074.9 63.9 %while.65 = (s32[]{:T(128)}, f32[16,8,256]{2,1,0:T(8,128)S(1)}, f32[16,8,256]{2,1,0:T(8,128)S(1)}, s32[16]{0:T(128)S(1)}, pred[128,256]{1,0:T(8,128)(4,1)S(1)}, ...) while((s32[]{:T(128)}, f32[16,8,256]{2,1,0:T(8,128)S(1)}, ...), condition=%wide.region_31.35_spmd, body=%wide.region_28.34_spmd.sunk | while | flops 38793220 | bytes 4596947 | solution.py:129
  1076.2 2.1 fusion.118
  1080.2 2.1 fusion.118
  1120.1 2.1 fusion.118
  1124.1 2.1 fusion.118
  1128.1 2.1 fusion.118
  1132.1 2.1 fusion.118
  1136.1 2.1 fusion.118
  1138.9 5.3 select_reduce_fusion.5
  1145.5 140.0 %all-reduce.24.cloned.1.call-done = f32[128,256]{1,0:T(8,128)} async-done(((f32[128,256]{1,0:T(8,128)}), f32[128,256]{1,0:T(8,128)}) %all-reduce.24.cloned.1.call-update) | async-done | bytes 131088 | tf_op jit(solution)/shard_map/pmax | solution.py:159
  1287.8 143.8 %all-reduce.26.cloned.1.call-done = f32[128,256]{1,0:T(8,128)} async-done(((f32[128,256]{1,0:T(8,128)}), f32[128,256]{1,0:T(8,128)}) %all-reduce.26.cloned.1.call-update) | async-done | bytes 131088 | tf_op jit(solution)/shard_map/psum | solution.py:162
  1433.5 108.6 %while.66 = (s32[]{:T(128)}, f32[16,8,256]{2,1,0:T(8,128)S(1)}, f32[16,8,256]{2,1,0:T(8,128)S(1)}, f32[16,32,8,256]{3,1,2,0:T(8,128)}, s32[16]{0:T(128)S(1)}, /*...) while((s32[]{:T(128)}, f32[16,8,256]{2,1,0:T(8,128)S(1)}, ...), condition=%wide.region_38.42_spmd, body=%wide.region_35.41_spmd.sunk | while | flops 241168384 | bytes 7098079 | solution.py:129
  1434.8 2.1 fusion.120
  1437.0 2.8 fusion.122
  1443.7 2.8 fusion.122
  1450.5 2.8 fusion.122
  1457.3 2.8 fusion.122
  1464.1 2.8 fusion.122
  1470.9 2.8 fusion.122
  1475.6 2.1 fusion.120
  1477.7 2.8 fusion.122
  1484.5 2.8 fusion.122
  1489.1 2.1 fusion.120
  1491.3 2.8 fusion.122
  1498.1 2.8 fusion.122
  1502.7 2.1 fusion.120
  1504.9 2.8 fusion.122
  1511.7 2.8 fusion.122
  1518.5 2.8 fusion.122
  1523.1 2.1 fusion.120
  1525.2 2.8 fusion.122
  1529.9 2.1 fusion.120
  1532.0 2.8 fusion.122
  1536.6 2.1 fusion.120
  1538.8 2.8 fusion.122
  1542.2 4.7 select_reduce_fusion.4
  1547.8 5.2 broadcast_multiply_fusion
  1553.0 130.9 %all-reduce.28.cloned.1.call-done = f32[128,256]{1,0:T(8,128)} async-done(((f32[128,256]{1,0:T(8,128)}), f32[128,256]{1,0:T(8,128)}) %all-reduce.28.cloned.1.call-update) | async-done | bytes 131088 | tf_op jit(solution)/shard_map/pmax | solution.py:175
  1686.0 9.2 bitcast_multiply_fusion
  1695.2 5.4 copy.50
  1702.1 204.2 %all-reduce.30.cloned.1.call-done = (f32[32,32768]{1,0:T(8,128)}, f32[32768]{0:T(1024)}) async-done(((f32[32,32768]{1,0:T(8,128)}, f32[32768]{0:T(1024)}), (f32[32,32768]{1,0:T(8,128)}, f32[32768]{0:T(1024)})) %all-reduce.30.cloned.1.call-update) | async-done | bytes 4325392 | tf_op jit(solution)/shard_map/psum | solution.py:180
  (729 shorter events, 252.6 us)
Async XLA Ops:
  7.2 4.4 copy-start
  7.2 223.4 %all-reduce.12.cloned.1.call-start = ((), (), s32[]{:S(2)}) async-start(), calls=%async_computation | async-start | bytes 262144 | tf_op jit(solution)/shard_map/pmax | solution.py:147
  16.3 2.4 copy-start.3
  18.7 1.6 copy-start.7
  25.8 67.2 %copy-start.4 = (f32[32768]{0:T(1024)S(1)}, f32[32768]{0:T(1024)}, u32[]{:S(2)}) copy-start(f32[32768]{0:T(1024)} %param.25) | copy-start | bytes 393220
  25.8 67.3 %copy-start.6 = (s32[128]{0:T(128)S(1)}, s32[128]{0:T(128)}, u32[]{:S(2)}) copy-start(s32[128]{0:T(128)} %param.27) | copy-start | bytes 1540
  93.0 275.8 %all-reduce.14.cloned.1.call-start = ((), (), s32[]{:S(2)}) async-start(), calls=%async_computation.1 | async-start | bytes 262144 | tf_op jit(solution)/shard_map/psum | solution.py:150
  232.4 348.9 %all-reduce.16.cloned.1.call-start = ((), (), s32[]{:S(2)}) async-start(), calls=%async_computation.2 | async-start | bytes 262144 | tf_op jit(solution)/shard_map/pmax | solution.py:159
  370.8 212.5 %copy-start.5 = (f32[32768]{0:T(1024)S(1)}, f32[32768]{0:T(1024)}, u32[]{:S(2)}) copy-start(f32[32768]{0:T(1024)} %param.26) | copy-start | bytes 393220
  440.1 287.2 %all-reduce.18.cloned.1.call-start = ((), (), s32[]{:S(2)}) async-start(), calls=%async_computation.3 | async-start | bytes 262144 | tf_op jit(solution)/shard_map/psum | solution.py:162
  583.2 351.6 %all-reduce.20.cloned.1.call-start = ((), (), s32[]{:S(2)}) async-start(), calls=%async_computation.4 | async-start | bytes 262144 | tf_op jit(solution)/shard_map/pmax | solution.py:147
  798.5 274.4 %all-reduce.22.cloned.1.call-start = ((), (), s32[]{:S(2)}) async-start(), calls=%async_computation.5 | async-start | bytes 262144 | tf_op jit(solution)/shard_map/psum | solution.py:150
  936.7 348.8 %all-reduce.24.cloned.1.call-start = ((), (), s32[]{:S(2)}) async-start(), calls=%async_computation.6 | async-start | bytes 262144 | tf_op jit(solution)/shard_map/pmax | solution.py:159
  1144.2 287.3 %all-reduce.26.cloned.1.call-start = ((), (), s32[]{:S(2)}) async-start(), calls=%async_computation.7 | async-start | bytes 262144 | tf_op jit(solution)/shard_map/psum | solution.py:162
  1287.4 396.5 %all-reduce.28.cloned.1.call-start = ((), (), s32[]{:S(2)}) async-start(), calls=%async_computation.8 | async-start | bytes 262144 | tf_op jit(solution)/shard_map/pmax | solution.py:175
  1546.9 0.7 copy-start.1
  1547.6 358.7 %all-reduce.30.cloned.1.call-start = ((), (), s32[]{:S(2)}) async-start(), calls=%async_computation.9 | async-start | bytes 8650752 | tf_op jit(solution)/shard_map/psum | solution.py:180
  1547.8 136.1 %copy-start.2 = (f32[128,256]{1,0:T(8,128)S(1)}, f32[128,256]{1,0:T(8,128)}, u32[]{:S(2)}) copy-start(f32[128,256]{1,0:T(8,128)} %copy-done.1) | copy-start | bytes 393220
Sparse Core Ops, SparseCore 0:
  93.1 137.4 all-reduce.11
  233.9 134.8 all-reduce.13
  440.2 141.1 all-reduce.15
  584.6 142.6 all-reduce.17
  798.6 136.1 all-reduce.19
  938.1 134.8 all-reduce.21
  1144.3 141.1 all-reduce.23
  1288.9 142.6 all-reduce.25
  1547.7 136.1 all-reduce.27
  1700.7 205.5 all-reduce.29
where the time goes:
time: 1920 us
  waiting for transfers between devices  1450 us (76%)
  matrix products  236 us (12%)
  other arithmetic  85.8 us (4%)
  local copies, waits for them, and re-layouts  74.4 us (4%)
  loops' own time  58 us (3%)
    psum x2, waiting for transfers between devices, shards(): lax.psum(summed * jnp.exp(highest - target_global_max), 'src')  288 us
    pmax x2, waiting for transfers between devices, shards(): target_global_max = lax.pmax(highest, 'src')  280 us
    psum x2, waiting for transfers between devices, shards(): lax.psum(summed * jnp.exp(highest - source_global_max), 'tgt')  272 us
    pmax x2, waiting for transfers between devices, shards(): source_global_max = lax.pmax(highest, 'tgt')  270 us
    psum x1, waiting for transfers between devices, shards(): numerator, denominator = lax.psum((numerator, denominator), 'tgt')  204 us
    dot_general x80, matrix products, one_group(): jnp.einsum('dpi,dpj->pij', src_part, tgt_part, preferred_element_type=jnp...  169 us
    pmax x1, waiting for transfers between devices, shards(): global_max = lax.pmax(highest, 'tgt')  131 us
    another operation x5, loops' own time, tile_sweep(): results = lax.map(one_group, jnp.arange(group_count, dtype=jnp.int32))  58 us
  transfers between devices with their start and end apart: 10, of which 10 were waited for; matrix products, arithmetic and copies ran while one was open for 1% of the time, Pallas kernels for 0%

commit v1 on v0

v1 whole, which is shorter than its diff:
```python
import functools

import jax
import jax.numpy as jnp
from jax import lax
from jax.experimental import pallas as pl
from jax.experimental.pallas import tpu as pltpu
from jax.sharding import PartitionSpec as P

ITERS = 2
MESH = pl.DeviceIdType.MESH
EMPTY = -1e30
TILE = 256
SUB = 8
AUX = 16
MAPROWS = 40
MIB = 1 << 20


def split3(row):
    high = row.astype(jnp.bfloat16).astype(jnp.float32)
    rest = row - high
    mid = rest.astype(jnp.bfloat16).astype(jnp.float32)
    low = rest - mid
    return high, mid, low


def cluster_row(ref, cluster):
    first = ref[pl.ds(2 * cluster, 1), :]
    second = ref[pl.ds(2 * cluster + 1, 1), :]
    return jnp.concatenate([first, second], axis=1)


def aux_rows(row, offset, other):
    at = lax.broadcasted_iota(jnp.int32, (AUX, TILE), 0)
    high, mid, low = split3(row)
    out = jnp.where((at >= other) & (at < other + 3), 1.0, 0.0)
    out = jnp.where(at == offset, high, out)
    out = jnp.where(at == offset + 1, mid, out)
    out = jnp.where(at == offset + 2, low, out)
    return out.astype(jnp.bfloat16)


def cells_of(ref, cluster):
    return ref[:, pl.ds(pl.multiple_of(cluster * TILE, TILE), TILE)]


def sweep_kernel(kind, sub_ids, lane_ids, count, sub_cells, lane_cells, sub_pot, lane_pot, out, *scratch):
    clusters = lane_cells.shape[1] // TILE
    if kind == "max":
        top, total = scratch
        top[...] = jnp.full(top.shape, EMPTY, jnp.float32)
        total[...] = jnp.zeros(total.shape, jnp.float32)
    elif kind == "sum":
        (total,) = scratch
        total[...] = jnp.zeros(total.shape, jnp.float32)
    else:
        out[...] = jnp.zeros(out.shape, jnp.float32)

    def tile(p):
        a, b = sub_ids[p], lane_ids[p]
        sub = cells_of(sub_cells, a)
        lane = cells_of(lane_cells, b)
        sub_aux = aux_rows(cluster_row(sub_pot, a), 0, 3)
        lane_aux = aux_rows(cluster_row(lane_pot, b), 3, 0)
        left = jnp.concatenate([sub, sub_aux], axis=0)
        right = jnp.concatenate([lane * jnp.bfloat16(4.0), lane_aux], axis=0)
        score = lax.dot_general(left, right, (((0,), (0,)), ((), ())), preferred_element_type=jnp.float32)
        if kind == "max":
            score = score.reshape(TILE // SUB, SUB, TILE)
            old = top[b]
            new = jnp.maximum(old, jnp.max(score, axis=0))
            part = jnp.sum(jnp.exp(score - new[None]), axis=0)
            total[b] = total[b] * jnp.exp(old - new) + part
            top[b] = new
        elif kind == "sum":
            weight = jnp.exp(score).reshape(TILE // SUB, SUB, TILE)
            total[b] = total[b] + jnp.sum(weight, axis=0)
        else:
            weight = jnp.exp(score)
            high = weight.astype(jnp.bfloat16)
            low = (weight - high.astype(jnp.float32)).astype(jnp.bfloat16)
            ones = jnp.where(lax.broadcasted_iota(jnp.int32, (AUX, TILE), 0) == 0, 1.0, 0.0).astype(jnp.bfloat16)
            cells = jnp.concatenate([sub, ones], axis=0)
            moved = jnp.dot(cells, high, preferred_element_type=jnp.float32)
            moved = moved + jnp.dot(cells, low, preferred_element_type=jnp.float32)
            out[b] = out[b] + moved[:MAPROWS]

    pl.loop(0, count[0])(tile)

    if kind == "map":
        return

    per = out.shape[2] // 2

    def finish(c):
        shard, at = c // per, c % per
        if kind == "max":
            best = jnp.max(top[c], axis=0, keepdims=True)
            row = jnp.sum(total[c] * jnp.exp(top[c] - best), axis=0, keepdims=True)
            rows = (best, row)
        else:
            rows = (jnp.sum(total[c], axis=0, keepdims=True),)
        for q, value in enumerate(rows):
            out[shard, q, pl.ds(2 * at, 1), :] = value[:, :128]
            out[shard, q, pl.ds(2 * at + 1, 1), :] = value[:, 128:]

    pl.loop(0, clusters)(finish)


def sweep(kind, shards, sub_ids, lane_ids, count, sub_cells, lane_cells, sub_pot, lane_pot):
    clusters = lane_cells.shape[1] // TILE
    if kind == "map":
        out = jax.ShapeDtypeStruct((clusters, MAPROWS, TILE), jnp.float32)
        scratch = []
    else:
        many = 2 if kind == "max" else 1
        out = jax.ShapeDtypeStruct((shards, many, 2 * clusters // shards, 128), jnp.float32)
        scratch = [pltpu.VMEM((clusters, SUB, TILE), jnp.float32)] * many
    smem = pl.BlockSpec(memory_space=pltpu.SMEM)
    vmem = pl.BlockSpec(memory_space=pltpu.VMEM)
    return pl.pallas_call(
        functools.partial(sweep_kernel, kind),
        out_shape=out,
        in_specs=[smem] * 3 + [vmem] * 4,
        out_specs=vmem,
        scratch_shapes=scratch,
        compiler_params=pltpu.CompilerParams(vmem_limit_bytes=48 * MIB),
        name="sweep_" + kind,
    )(sub_ids, lane_ids, count, sub_cells, lane_cells, sub_pot, lane_pot)


def greet(axis, n):
    me = lax.axis_index(axis)
    barrier = pltpu.get_barrier_semaphore()
    for k in range(1, n):
        pl.semaphore_signal(barrier, inc=1, device_id={axis: lax.rem(me + k, n)}, device_id_type=MESH)
    pl.semaphore_wait(barrier, n - 1)
    return me


def reduce_kernel(kind, axis, n, part, old, logmass, out, held, send1, recv1, send2, recv2):
    me = greet(axis, n)
    rows = old.shape[0] // n
    copies = []
    for k in range(1, n):
        peer = lax.rem(me + k, n)
        copy = pltpu.make_async_remote_copy(
            src_ref=part.at[peer], dst_ref=held.at[k], send_sem=send1.at[k], recv_sem=recv1.at[k],
            device_id={axis: peer}, device_id_type=MESH)
        copy.start()
        copies.append(copy)
    for copy in copies:
        copy.wait()
    mine = pl.ds(pl.multiple_of(me * rows, rows), rows)
    if kind == "max":
        best = part[me, 0]
        for k in range(1, n):
            best = jnp.maximum(best, held[k, 0])
        total = part[me, 1] * jnp.exp(part[me, 0] - best)
        for k in range(1, n):
            total = total + held[k, 1] * jnp.exp(held[k, 0] - best)
        lse = best + jnp.log(total)
    else:
        total = part[me, 0]
        for k in range(1, n):
            total = total + held[k, 0]
        lse = jnp.log(jnp.where(total > 0.0, total, 1.0))
    mass = logmass[mine, :]
    out[mine, :] = jnp.where(mass > 0.5 * EMPTY, old[mine, :] + mass - lse, EMPTY)
    copies = []
    for k in range(1, n):
        peer = lax.rem(me + k, n)
        copy = pltpu.make_async_remote_copy(
            src_ref=out.at[mine], dst_ref=out.at[mine], send_sem=send2.at[k], recv_sem=recv2.at[k],
            device_id={axis: peer}, device_id_type=MESH)
        copy.start()
        copies.append(copy)
    for copy in copies:
        copy.wait()


def reduce(kind, axis, ident, part, old, logmass):
    n = part.shape[0]
    vmem = pl.BlockSpec(memory_space=pltpu.VMEM)
    return pl.pallas_call(
        functools.partial(reduce_kernel, kind, axis, n),
        out_shape=jax.ShapeDtypeStruct(old.shape, jnp.float32),
        in_specs=[vmem] * 3,
        out_specs=vmem,
        scratch_shapes=[pltpu.VMEM(part.shape, jnp.float32)] + [pltpu.SemaphoreType.DMA((n,))] * 4,
        compiler_params=pltpu.CompilerParams(collective_id=ident, has_side_effects=True, vmem_limit_bytes=32 * MIB),
        name="reduce_" + kind + "_" + axis,
    )(part, old, logmass)


def scatter_kernel(axis, n, moved, out, held, send, recv, own):
    me = greet(axis, n)
    per = moved.shape[0] // n
    copies = []
    for k in range(1, n):
        peer = lax.rem(me + k, n)
        copy = pltpu.make_async_remote_copy(
            src_ref=moved.at[pl.ds(peer * per, per)], dst_ref=held.at[k], send_sem=send.at[k], recv_sem=recv.at[k],
            device_id={axis: peer}, device_id_type=MESH)
        copy.start()
        copies.append(copy)
    local = pltpu.make_async_copy(moved.at[pl.ds(me * per, per)], held.at[0], own)
    local.start()
    local.wait()
    for copy in copies:
        copy.wait()

    features = out.shape[0]

    def one(c):
        total = held[0, c]
        for k in range(1, n):
            total = total + held[k, c]
        weight = total[features:features + 1]
        weight = jnp.where(weight > 0.0, weight, 1.0)
        out[:, pl.ds(pl.multiple_of(c * TILE, TILE), TILE)] = total[:features] / weight

    pl.loop(0, per)(one)


def scatter(axis, ident, n, features, moved):
    clusters = moved.shape[0]
    per = clusters // n
    return pl.pallas_call(
        functools.partial(scatter_kernel, axis, n),
        out_shape=jax.ShapeDtypeStruct((features, per * TILE), jnp.float32),
        in_specs=[pl.BlockSpec(memory_space=pl.ANY)],
        out_specs=pl.BlockSpec(memory_space=pltpu.VMEM),
        scratch_shapes=[
            pltpu.VMEM((n, per) + moved.shape[1:], jnp.float32),
            pltpu.SemaphoreType.DMA((n,)),
            pltpu.SemaphoreType.DMA((n,)),
            pltpu.SemaphoreType.DMA,
        ],
        compiler_params=pltpu.CompilerParams(collective_id=ident, has_side_effects=True, vmem_limit_bytes=48 * MIB),
        name="scatter",
    )(moved)


def pair_table(pair_lists, tgt_block, per_block, capacity):
    width = pair_lists.shape[1]
    flat = pair_lists.reshape(-1)
    chosen = flat // per_block == tgt_block
    rank = jnp.cumsum(chosen.astype(jnp.int32)) - 1
    slots = jnp.arange(capacity, dtype=jnp.int32)
    matches = (rank[None, :] == slots[:, None]) & chosen[None, :]
    sources = jnp.arange(flat.shape[0], dtype=jnp.int32) // width
    pair_src = jnp.sum(jnp.where(matches, sources[None, :], 0), axis=1)
    pair_tgt = jnp.sum(jnp.where(matches, (flat % per_block)[None, :], 0), axis=1)
    return pair_src, pair_tgt, jnp.sum(chosen.astype(jnp.int32)).reshape(1)


def side(cells, mass, count):
    clusters = count.shape[0]
    wide = cells.astype(jnp.float32)
    norm = jnp.sum(wide * wide, axis=0).reshape(2 * clusters, 128)
    place = jnp.arange(2, dtype=jnp.int32)[None, :, None] * 128 + jnp.arange(128, dtype=jnp.int32)[None, None, :]
    live = (place < count[:, None, None]).reshape(2 * clusters, 128)
    logmass = jnp.where(live, jnp.log(mass).reshape(2 * clusters, 128), EMPTY)
    return norm, live, logmass


def shards(source_cells, target_cells, source_mass, target_mass, source_count, target_count, pair_lists):
    features = source_cells.shape[0]
    n_src, n_tgt = lax.axis_size("src"), lax.axis_size("tgt")
    capacity = 2 * pair_lists.size // n_tgt
    own_src, own_tgt, own = pair_table(pair_lists, lax.axis_index("tgt"), target_count.shape[0], capacity)
    src_norm, src_live, src_logmass = side(source_cells, source_mass, source_count)
    tgt_norm, tgt_live, tgt_logmass = side(target_cells, target_mass, target_count)
    u = -2.0 * src_norm
    v = jnp.where(tgt_live, -2.0 * tgt_norm, EMPTY)
    for step in range(ITERS):
        kind = "max" if step == 0 else "sum"
        part = sweep(kind, n_tgt, own_tgt, own_src, own, target_cells, source_cells, v, u)
        u = reduce(kind, "tgt", 2 * step, part, u, src_logmass)
        part = sweep(kind, n_src, own_src, own_tgt, own, source_cells, target_cells, u, v)
        v = reduce(kind, "src", 2 * step + 1, part, v, tgt_logmass)
    moved = sweep("map", n_tgt, own_tgt, own_src, own, target_cells, source_cells, v, u)
    mapped = scatter("tgt", 2 * ITERS, n_tgt, features, moved)
    source_pot = jnp.where(src_live, 0.5 * u + src_norm, 0.0)
    target_pot = jnp.where(tgt_live, 0.5 * v + tgt_norm, 0.0)
    return source_pot.reshape(-1), target_pot.reshape(-1), mapped


def solution(mesh):
    return jax.shard_map(
        shards,
        mesh=mesh,
        in_specs=(P(None, "src"), P(None, "tgt"), P("src"), P("tgt"), P("src"), P("tgt"), P("src", None)),
        out_specs=(P("src"), P("tgt"), P(None, ("src", "tgt"))),
        check_vma=False,
    )
```

time: 1920 us -> 402 us (0.21)
  waiting for transfers between devices: 1450 us -> 0 us
  Pallas kernels: 0 us -> 381 us
  matrix products: 236 us -> 0 us
  other arithmetic: 85.8 us -> 7.69 us
  local copies, waits for them, and re-layouts: 74.4 us -> 6.16 us
  loops' own time: 58 us -> 0 us
    psum x5 -> x0, waiting for transfers between devices: 764 us -> none  [the longest x2 288 us: shards(): lax.psum(summed * jnp.exp(highest - target_global_max), 'src')]
    pmax x5 -> x0, waiting for transfers between devices: 681 us -> none  [the longest x2 280 us: shards(): target_global_max = lax.pmax(highest, 'src')]
    pallas_call x0 -> x10, Pallas kernels: none -> 381 us  [the longest x1 141 us: scatter(): pl.pallas_call(functools.partial(scatter_kernel, axis, n), out_shape=jax....]
    dot_general x107 -> x0, matrix products: 236 us -> none  [the longest x80 169 us: one_group(): jnp.einsum('dpi,dpj->pij', src_part, tgt_part, preferred_element_type=jnp...]
    another operation x5 -> x0, loops' own time: 58 us -> none  [tile_sweep(): results = lax.map(one_group, jnp.arange(group_count, dtype=jnp.int32))]
    dynamic_slice x384 -> x0, local copies, waits for them, and re-layouts: 49.9 us -> none  [the longest x80 46.9 us: tile_sweep(): results = lax.map(one_group, jnp.arange(group_count, dtype=jnp.int32))]
    reduce_sum x83 -> x4, other arithmetic: 43.7 us -> 6.27 us  [the longest x2 4.56 us: side(): norm = jnp.sum(wide * wide, axis=0).reshape(2 * clusters, 128)]
    reduce_max x5 -> x0, other arithmetic: 25.9 us -> none  [fold_tiles(): jnp.max(jnp.where(member[:, :, None] > 0.5, maxima[None], empty_peak), ax...]
  transfers between devices with their start and end apart: 10 -> 0, of which waited for: 10 -> 0; matrix products, arithmetic and copies ran while one was open for 1% -> 0% of each run, Pallas kernels for 0% -> 0%
where the time goes in v1:
time: 402 us; the launch traced here: 395 us
  Pallas kernels  381 us (95%)
  other arithmetic  7.69 us (2%)
  local copies, waits for them, and re-layouts  6.16 us (2%)
    pallas_call x1, Pallas kernels, scatter(): pl.pallas_call(functools.partial(scatter_kernel, axis, n), out_shape=jax....  141 us
    pallas_call x4, Pallas kernels, reduce(): pl.pallas_call(functools.partial(reduce_kernel, kind, axis, n), out_shape...  127 us
    pallas_call x5, Pallas kernels, sweep(): pl.pallas_call(functools.partial(sweep_kernel, kind), out_shape=out, in_s...  112 us

profile of v1, /device:TPU:24, one launch (start us, length us, event | category | flops | bytes accessed | tf_op | source)
XLA Modules:
  0.0 395.2 jit_solution(8454131418867317562)
XLA Ops:
  0.6 0.0 copy-start
  0.6 0.0 copy-start.3
  0.7 0.0 copy-start.4
  0.7 1.5 convert_reduce_fusion
  2.2 0.1 iota_add_fusion
  2.2 0.8 copy.13
  3.0 0.1 reshape.166
  3.1 0.1 reshape.164
  3.2 0.3 reduce-window.9
  3.5 0.1 slice.7
  3.6 0.1 slice_reduce_fusion
  3.7 0.1 add_bitcast_fusion
  3.8 0.2 select_reduce_fusion
  4.0 0.7 lt.48
  4.8 0.1 lt.49
  4.9 0.7 lt.53
  5.7 0.1 lt.54
  5.8 0.0 copy-start.1
  5.9 2.3 multiply_reduce_fusion
  8.2 2.2 multiply_reduce_fusion.1
  10.4 0.0 copy-done.3
  10.5 0.0 copy-done.4
  10.5 0.1 bitcast_select_fusion
  10.6 0.0 copy-done
  10.7 0.0 copy-done.1
  10.7 22.5 %sweep_max.2.part = f32[16,2,16,128]{3,2,1,0:T(8,128)S(1)} custom-call(s32[128]{0:T(128)S(1)} %get-tuple-element.4.sub_ids.lane_ids, s32[128]{0:T(128)S(1)} %get-tuple-element.3.lane_ids.sub_ids, s32[1]{0:T(128)} %bitcast.2.count, bf16[32,32768]{1,0:T(8,128)(2,1)S(1)} %copy-done.1, bf16[32,32768]{1,0:T(8,128)(2,1)S(1)} %copy-done, ...), custom_call_target="tpu_custom_call" | custom-call | tf_op jit(solution)/shard_map/sweep_max/pallas_call | solution.py:122
  33.1 37.5 %reduce_max_tgt.1.sub_pot.lane_pot.old = f32[256,128]{1,0:T(8,128)S(1)} custom-call(f32[16,2,16,128]{3,2,1,0:T(8,128)S(1)} %sweep_max.2.part, f32[256,128]{1,0:T(8,128)S(1)} %bitcast_multiply_fusion.lane_pot.old, f32[256,128]{1,0:T(8,128)S(1)} %get-tuple-element.9.logmass), custom_call_target="tpu_custom_call" | custom-call | tf_op jit(solution)/shard_map/reduce_max_tgt/pallas_call | solution.py:186
  70.7 22.5 %sweep_max.3.part = f32[16,2,16,128]{3,2,1,0:T(8,128)S(1)} custom-call(s32[128]{0:T(128)S(1)} %get-tuple-element.3.lane_ids.sub_ids, s32[128]{0:T(128)S(1)} %get-tuple-element.4.sub_ids.lane_ids, s32[1]{0:T(128)} %bitcast.2.count, bf16[32,32768]{1,0:T(8,128)(2,1)S(1)} %copy-done, bf16[32,32768]{1,0:T(8,128)(2,1)S(1)} %copy-done.1, ...), custom_call_target="tpu_custom_call" | custom-call | tf_op jit(solution)/shard_map/sweep_max/pallas_call | solution.py:122
  93.1 32.3 %reduce_max_src.1.sub_pot.lane_pot.old = f32[256,128]{1,0:T(8,128)S(1)} custom-call(f32[16,2,16,128]{3,2,1,0:T(8,128)S(1)} %sweep_max.3.part, f32[256,128]{1,0:T(8,128)S(1)} %fusion.3.sub_pot.lane_pot.old, f32[256,128]{1,0:T(8,128)S(1)} %get-tuple-element.5.logmass), custom_call_target="tpu_custom_call" | custom-call | tf_op jit(solution)/shard_map/reduce_max_src/pallas_call | solution.py:186
  125.4 18.4 %sweep_sum.2.part = f32[16,1,16,128]{3,2,1,0:T(8,128)S(1)} custom-call(s32[128]{0:T(128)S(1)} %get-tuple-element.4.sub_ids.lane_ids, s32[128]{0:T(128)S(1)} %get-tuple-element.3.lane_ids.sub_ids, s32[1]{0:T(128)} %bitcast.2.count, bf16[32,32768]{1,0:T(8,128)(2,1)S(1)} %copy-done.1, bf16[32,32768]{1,0:T(8,128)(2,1)S(1)} %copy-done, ...), custom_call_target="tpu_custom_call" | custom-call | tf_op jit(solution)/shard_map/sweep_sum/pallas_call | solution.py:122
  143.8 31.9 %reduce_sum_tgt.1.sub_pot.lane_pot = f32[256,128]{1,0:T(8,128)S(1)} custom-call(f32[16,1,16,128]{3,2,1,0:T(8,128)S(1)} %sweep_sum.2.part, f32[256,128]{1,0:T(8,128)S(1)} %reduce_max_tgt.1.sub_pot.lane_pot.old, f32[256,128]{1,0:T(8,128)S(1)} %get-tuple-element.9.logmass), custom_call_target="tpu_custom_call" | custom-call | tf_op jit(solution)/shard_map/reduce_sum_tgt/pallas_call | solution.py:186
  175.7 18.4 %sweep_sum.3.part = f32[16,1,16,128]{3,2,1,0:T(8,128)S(1)} custom-call(s32[128]{0:T(128)S(1)} %get-tuple-element.3.lane_ids.sub_ids, s32[128]{0:T(128)S(1)} %get-tuple-element.4.sub_ids.lane_ids, s32[1]{0:T(128)} %bitcast.2.count, bf16[32,32768]{1,0:T(8,128)(2,1)S(1)} %copy-done, bf16[32,32768]{1,0:T(8,128)(2,1)S(1)} %copy-done.1, ...), custom_call_target="tpu_custom_call" | custom-call | tf_op jit(solution)/shard_map/sweep_sum/pallas_call | solution.py:122
  194.0 25.5 %reduce_sum_src.1.sub_pot = f32[256,128]{1,0:T(8,128)S(1)} custom-call(f32[16,1,16,128]{3,2,1,0:T(8,128)S(1)} %sweep_sum.3.part, f32[256,128]{1,0:T(8,128)S(1)} %reduce_max_src.1.sub_pot.lane_pot.old, f32[256,128]{1,0:T(8,128)S(1)} %get-tuple-element.5.logmass), custom_call_target="tpu_custom_call" | custom-call | tf_op jit(solution)/shard_map/reduce_sum_src/pallas_call | solution.py:186
  219.6 0.8 fusion.2
  220.4 30.4 %sweep_map.1.moved = f32[128,40,256]{2,1,0:T(8,128)} custom-call(s32[128]{0:T(128)S(1)} %get-tuple-element.4.sub_ids.lane_ids, s32[128]{0:T(128)S(1)} %get-tuple-element.3.lane_ids.sub_ids, s32[1]{0:T(128)} %bitcast.2.count, bf16[32,32768]{1,0:T(8,128)(2,1)S(1)} %copy-done.1, bf16[32,32768]{1,0:T(8,128)(2,1)S(1)} %copy-done, ...), custom_call_target="tpu_custom_call" | custom-call | tf_op jit(solution)/shard_map/sweep_map/pallas_call | solution.py:122
  250.8 0.0 copy-start.2
  250.8 2.5 copy-done.2
  253.3 141.2 %scatter.1 = f32[32,2048]{1,0:T(8,128)S(1)} custom-call(f32[128,40,256]{2,1,0:T(8,128)S(1)} %copy-done.2), custom_call_target="tpu_custom_call" | custom-call | tf_op jit(solution)/shard_map/scatter/pallas_call | solution.py:230
  394.5 0.7 copy.16
  (9 shorter events, 0.1 us)
Async XLA Ops:
  0.6 10.0 %copy-start = (bf16[32,32768]{1,0:T(8,128)(2,1)S(1)}, bf16[32,32768]{1,0:T(8,128)(2,1)}, u32[]{:S(2)}) copy-start(bf16[32,32768]{1,0:T(8,128)(2,1)} %lane_cells.9) | copy-start | bytes 6291460
  0.6 9.8 %copy-start.3 = (f32[32768]{0:T(1024)S(1)}, f32[32768]{0:T(1024)}, u32[]{:S(2)}) copy-start(f32[32768]{0:T(1024)} %param.10) | copy-start | bytes 393220
  0.7 9.8 %copy-start.4 = (f32[32768]{0:T(1024)S(1)}, f32[32768]{0:T(1024)}, u32[]{:S(2)}) copy-start(f32[32768]{0:T(1024)} %param.9) | copy-start | bytes 393220
  5.8 4.8 %copy-start.1 = (bf16[32,32768]{1,0:T(8,128)(2,1)S(1)}, bf16[32,32768]{1,0:T(8,128)(2,1)}, u32[]{:S(2)}) copy-start(bf16[32,32768]{1,0:T(8,128)(2,1)} %sub_cells.9) | copy-start | bytes 6291460
  250.8 2.5 copy-start.2

commit v2 on v1

--- a/solution.py
+++ b/solution.py
@@ -1,4 +1,5 @@
 import functools
+import math
 
 import jax
 import jax.numpy as jnp
@@ -45,7 +46,7 @@
     return ref[:, pl.ds(pl.multiple_of(cluster * TILE, TILE), TILE)]
 
 
-def sweep_kernel(kind, sub_ids, lane_ids, count, sub_cells, lane_cells, sub_pot, lane_pot, out, *scratch):
+def sweep_kernel(kind, step, sub_ids, lane_ids, count, sub_cells, lane_cells, sub_pot, lane_pot, out, *scratch):
     clusters = lane_cells.shape[1] // TILE
     if kind == "max":
         top, total = scratch
@@ -86,26 +87,33 @@
             moved = moved + jnp.dot(cells, low, preferred_element_type=jnp.float32)
             out[b] = out[b] + moved[:MAPROWS]
 
-    pl.loop(0, count[0])(tile)
+    def group(g):
+        for r in range(step):
+            tile(g * step + r)
+
+    pl.loop(0, count[0] // step)(group)
 
     if kind == "map":
         return
 
-    per = out.shape[2] // 2
+    per = out.shape[1] // 2
 
     def finish(c):
         shard, at = c // per, c % per
         if kind == "max":
             best = jnp.max(top[c], axis=0, keepdims=True)
             row = jnp.sum(total[c] * jnp.exp(top[c] - best), axis=0, keepdims=True)
-            rows = (best, row)
+            value = best + jnp.log(jnp.where(row > 0.0, row, 1.0))
         else:
-            rows = (jnp.sum(total[c], axis=0, keepdims=True),)
-        for q, value in enumerate(rows):
-            out[shard, q, pl.ds(2 * at, 1), :] = value[:, :128]
-            out[shard, q, pl.ds(2 * at + 1, 1), :] = value[:, 128:]
-
-    pl.loop(0, clusters)(finish)
+            value = jnp.sum(total[c], axis=0, keepdims=True)
+        out[shard, pl.ds(2 * at, 1), :] = value[:, :128]
+        out[shard, pl.ds(2 * at + 1, 1), :] = value[:, 128:]
+
+    def finish_group(g):
+        for r in range(8):
+            finish(g * 8 + r)
+
+    pl.loop(0, clusters // 8)(finish_group)
 
 
 def sweep(kind, shards, sub_ids, lane_ids, count, sub_cells, lane_cells, sub_pot, lane_pot):
@@ -115,12 +123,12 @@
         scratch = []
     else:
         many = 2 if kind == "max" else 1
-        out = jax.ShapeDtypeStruct((shards, many, 2 * clusters // shards, 128), jnp.float32)
+        out = jax.ShapeDtypeStruct((shards, 2 * clusters // shards, 128), jnp.float32)
         scratch = [pltpu.VMEM((clusters, SUB, TILE), jnp.float32)] * many
     smem = pl.BlockSpec(memory_space=pltpu.SMEM)
     vmem = pl.BlockSpec(memory_space=pltpu.VMEM)
     return pl.pallas_call(
-        functools.partial(sweep_kernel, kind),
+        functools.partial(sweep_kernel, kind, math.gcd(sub_ids.shape[0] // 2, 16)),
         out_shape=out,
         in_specs=[smem] * 3 + [vmem] * 4,
         out_specs=vmem,
@@ -154,17 +162,17 @@
         copy.wait()
     mine = pl.ds(pl.multiple_of(me * rows, rows), rows)
     if kind == "max":
-        best = part[me, 0]
+        best = part[me]
         for k in range(1, n):
-            best = jnp.maximum(best, held[k, 0])
-        total = part[me, 1] * jnp.exp(part[me, 0] - best)
+            best = jnp.maximum(best, held[k])
+        total = jnp.exp(part[me] - best)
         for k in range(1, n):
-            total = total + held[k, 1] * jnp.exp(held[k, 0] - best)
+            total = total + jnp.exp(held[k] - best)
         lse = best + jnp.log(total)
     else:
-        total = part[me, 0]
+        total = part[me]
         for k in range(1, n):
-            total = total + held[k, 0]
+            total = total + held[k]
         lse = jnp.log(jnp.where(total > 0.0, total, 1.0))
     mass = logmass[mine, :]
     out[mine, :] = jnp.where(mass > 0.5 * EMPTY, old[mine, :] + mass - lse, EMPTY)

time: 402 us -> 259 us (0.64); the launches traced: 395 us -> 257 us
  Pallas kernels: 381 us -> 242 us
    pallas_call x5, Pallas kernels: 112 us -> 35.8 us  [sweep(): pl.pallas_call(functools.partial(sweep_kernel, kind, math.gcd(sub_ids.sha...]
    pallas_call x4, Pallas kernels: 127 us -> 77.2 us  [reduce(): pl.pallas_call(functools.partial(reduce_kernel, kind, axis, n), out_shape...]
    pallas_call x1, Pallas kernels: 141 us -> 129 us  [scatter(): pl.pallas_call(functools.partial(scatter_kernel, axis, n), out_shape=jax....]
where the time goes in v2:
time: 259 us; the launch traced here: 257 us
  Pallas kernels  242 us (93%)
  other arithmetic  7.69 us (3%)
  local copies, waits for them, and re-layouts  6.16 us (2%)
    pallas_call x1, Pallas kernels, scatter(): pl.pallas_call(functools.partial(scatter_kernel, axis, n), out_shape=jax....  129 us
    pallas_call x4, Pallas kernels, reduce(): pl.pallas_call(functools.partial(reduce_kernel, kind, axis, n), out_shape...  77.2 us
    pallas_call x5, Pallas kernels, sweep(): pl.pallas_call(functools.partial(sweep_kernel, kind, math.gcd(sub_ids.sha...  35.8 us

profile of v2, /device:TPU:24, one launch (start us, length us, event | category | flops | bytes accessed | tf_op | source)
XLA Modules:
  0.0 256.6 jit_solution(16140649478961478269)
XLA Ops:
  0.6 0.0 copy-start
  0.6 0.0 copy-start.3
  0.7 0.0 copy-start.4
  0.7 1.5 convert_reduce_fusion
  2.2 0.1 iota_add_fusion
  2.2 0.8 copy.13
  3.0 0.1 reshape.166
  3.1 0.1 reshape.164
  3.2 0.3 reduce-window.9
  3.5 0.1 slice.7
  3.6 0.1 slice_reduce_fusion
  3.7 0.1 add_bitcast_fusion
  3.8 0.2 select_reduce_fusion
  4.0 0.7 lt.48
  4.8 0.1 lt.49
  4.9 0.7 lt.53
  5.7 0.1 lt.54
  5.8 0.0 copy-start.1
  5.9 2.3 multiply_reduce_fusion
  8.2 2.2 multiply_reduce_fusion.1
  10.4 0.0 copy-done.3
  10.5 0.0 copy-done.4
  10.5 0.1 bitcast_select_fusion
  10.6 0.0 copy-done
  10.7 0.0 copy-done.1
  10.7 7.5 %sweep_max.2.part = f32[16,16,128]{2,1,0:T(8,128)S(1)} custom-call(s32[128]{0:T(128)S(1)} %get-tuple-element.4.sub_ids.lane_ids, s32[128]{0:T(128)S(1)} %get-tuple-element.3.lane_ids.sub_ids, s32[1]{0:T(128)} %bitcast.2.count, bf16[32,32768]{1,0:T(8,128)(2,1)S(1)} %copy-done.1, bf16[32,32768]{1,0:T(8,128)(2,1)S(1)} %copy-done, ...), custom_call_target="tpu_custom_call" | custom-call | tf_op jit(solution)/shard_map/sweep_max/pallas_call | solution.py:130
  18.1 22.9 %reduce_max_tgt.1.sub_pot.lane_pot.old = f32[256,128]{1,0:T(8,128)S(1)} custom-call(f32[16,16,128]{2,1,0:T(8,128)S(1)} %sweep_max.2.part, f32[256,128]{1,0:T(8,128)S(1)} %bitcast_multiply_fusion.lane_pot.old, f32[256,128]{1,0:T(8,128)S(1)} %get-tuple-element.9.logmass), custom_call_target="tpu_custom_call" | custom-call | tf_op jit(solution)/shard_map/reduce_max_tgt/pallas_call | solution.py:194
  41.1 7.5 %sweep_max.3.part = f32[16,16,128]{2,1,0:T(8,128)S(1)} custom-call(s32[128]{0:T(128)S(1)} %get-tuple-element.3.lane_ids.sub_ids, s32[128]{0:T(128)S(1)} %get-tuple-element.4.sub_ids.lane_ids, s32[1]{0:T(128)} %bitcast.2.count, bf16[32,32768]{1,0:T(8,128)(2,1)S(1)} %copy-done, bf16[32,32768]{1,0:T(8,128)(2,1)S(1)} %copy-done.1, ...), custom_call_target="tpu_custom_call" | custom-call | tf_op jit(solution)/shard_map/sweep_max/pallas_call | solution.py:130
  48.5 16.6 %reduce_max_src.1.sub_pot.lane_pot.old = f32[256,128]{1,0:T(8,128)S(1)} custom-call(f32[16,16,128]{2,1,0:T(8,128)S(1)} %sweep_max.3.part, f32[256,128]{1,0:T(8,128)S(1)} %fusion.3.sub_pot.lane_pot.old, f32[256,128]{1,0:T(8,128)S(1)} %get-tuple-element.5.logmass), custom_call_target="tpu_custom_call" | custom-call | tf_op jit(solution)/shard_map/reduce_max_src/pallas_call | solution.py:194
  65.2 5.4 %sweep_sum.2.part = f32[16,16,128]{2,1,0:T(8,128)S(1)} custom-call(s32[128]{0:T(128)S(1)} %get-tuple-element.4.sub_ids.lane_ids, s32[128]{0:T(128)S(1)} %get-tuple-element.3.lane_ids.sub_ids, s32[1]{0:T(128)} %bitcast.2.count, bf16[32,32768]{1,0:T(8,128)(2,1)S(1)} %copy-done.1, bf16[32,32768]{1,0:T(8,128)(2,1)S(1)} %copy-done, ...), custom_call_target="tpu_custom_call" | custom-call | tf_op jit(solution)/shard_map/sweep_sum/pallas_call | solution.py:130
  70.6 19.8 %reduce_sum_tgt.1.sub_pot.lane_pot = f32[256,128]{1,0:T(8,128)S(1)} custom-call(f32[16,16,128]{2,1,0:T(8,128)S(1)} %sweep_sum.2.part, f32[256,128]{1,0:T(8,128)S(1)} %reduce_max_tgt.1.sub_pot.lane_pot.old, f32[256,128]{1,0:T(8,128)S(1)} %get-tuple-element.9.logmass), custom_call_target="tpu_custom_call" | custom-call | tf_op jit(solution)/shard_map/reduce_sum_tgt/pallas_call | solution.py:194
  90.5 5.4 %sweep_sum.3.part = f32[16,16,128]{2,1,0:T(8,128)S(1)} custom-call(s32[128]{0:T(128)S(1)} %get-tuple-element.3.lane_ids.sub_ids, s32[128]{0:T(128)S(1)} %get-tuple-element.4.sub_ids.lane_ids, s32[1]{0:T(128)} %bitcast.2.count, bf16[32,32768]{1,0:T(8,128)(2,1)S(1)} %copy-done, bf16[32,32768]{1,0:T(8,128)(2,1)S(1)} %copy-done.1, ...), custom_call_target="tpu_custom_call" | custom-call | tf_op jit(solution)/shard_map/sweep_sum/pallas_call | solution.py:130
  95.9 17.8 %reduce_sum_src.1.sub_pot = f32[256,128]{1,0:T(8,128)S(1)} custom-call(f32[16,16,128]{2,1,0:T(8,128)S(1)} %sweep_sum.3.part, f32[256,128]{1,0:T(8,128)S(1)} %reduce_max_src.1.sub_pot.lane_pot.old, f32[256,128]{1,0:T(8,128)S(1)} %get-tuple-element.5.logmass), custom_call_target="tpu_custom_call" | custom-call | tf_op jit(solution)/shard_map/reduce_sum_src/pallas_call | solution.py:194
  113.7 0.8 fusion.2
  114.5 10.0 %sweep_map.1.moved = f32[128,40,256]{2,1,0:T(8,128)} custom-call(s32[128]{0:T(128)S(1)} %get-tuple-element.4.sub_ids.lane_ids, s32[128]{0:T(128)S(1)} %get-tuple-element.3.lane_ids.sub_ids, s32[1]{0:T(128)} %bitcast.2.count, bf16[32,32768]{1,0:T(8,128)(2,1)S(1)} %copy-done.1, bf16[32,32768]{1,0:T(8,128)(2,1)S(1)} %copy-done, ...), custom_call_target="tpu_custom_call" | custom-call | tf_op jit(solution)/shard_map/sweep_map/pallas_call | solution.py:130
  124.5 0.0 copy-start.2
  124.5 2.5 copy-done.2
  127.0 128.9 %scatter.1 = f32[32,2048]{1,0:T(8,128)S(1)} custom-call(f32[128,40,256]{2,1,0:T(8,128)S(1)} %copy-done.2), custom_call_target="tpu_custom_call" | custom-call | tf_op jit(solution)/shard_map/scatter/pallas_call | solution.py:238
  255.9 0.7 copy.16
  (9 shorter events, 0.1 us)
Async XLA Ops:
  0.6 10.0 %copy-start = (bf16[32,32768]{1,0:T(8,128)(2,1)S(1)}, bf16[32,32768]{1,0:T(8,128)(2,1)}, u32[]{:S(2)}) copy-start(bf16[32,32768]{1,0:T(8,128)(2,1)} %lane_cells.9) | copy-start | bytes 6291460
  0.6 9.8 %copy-start.3 = (f32[32768]{0:T(1024)S(1)}, f32[32768]{0:T(1024)}, u32[]{:S(2)}) copy-start(f32[32768]{0:T(1024)} %param.10) | copy-start | bytes 393220
  0.7 9.8 %copy-start.4 = (f32[32768]{0:T(1024)S(1)}, f32[32768]{0:T(1024)}, u32[]{:S(2)}) copy-start(f32[32768]{0:T(1024)} %param.9) | copy-start | bytes 393220
  5.8 4.8 %copy-start.1 = (bf16[32,32768]{1,0:T(8,128)(2,1)S(1)}, bf16[32,32768]{1,0:T(8,128)(2,1)}, u32[]{:S(2)}) copy-start(bf16[32,32768]{1,0:T(8,128)(2,1)} %sub_cells.9) | copy-start | bytes 6291460
  124.5 2.5 copy-start.2

commit v3 on v2

--- a/solution.py
+++ b/solution.py
@@ -14,7 +14,6 @@
 TILE = 256
 SUB = 8
 AUX = 16
-MAPROWS = 40
 MIB = 1 << 20
 
 
@@ -56,7 +55,10 @@
         (total,) = scratch
         total[...] = jnp.zeros(total.shape, jnp.float32)
     else:
+        (den,) = scratch
+        features, per = out.shape[1], den.shape[1]
         out[...] = jnp.zeros(out.shape, jnp.float32)
+        den[...] = jnp.zeros(den.shape, jnp.float32)
 
     def tile(p):
         a, b = sub_ids[p], lane_ids[p]
@@ -85,7 +87,9 @@
             cells = jnp.concatenate([sub, ones], axis=0)
             moved = jnp.dot(cells, high, preferred_element_type=jnp.float32)
             moved = moved + jnp.dot(cells, low, preferred_element_type=jnp.float32)
-            out[b] = out[b] + moved[:MAPROWS]
+            out[b] = out[b] + moved[:features]
+            place = (b // per, pl.ds(b % per, 1))
+            den[place] = den[place] + moved[features:features + 1]
 
     def group(g):
         for r in range(step):
@@ -119,7 +123,10 @@
 def sweep(kind, shards, sub_ids, lane_ids, count, sub_cells, lane_cells, sub_pot, lane_pot):
     clusters = lane_cells.shape[1] // TILE
     if kind == "map":
-        out = jax.ShapeDtypeStruct((clusters, MAPROWS, TILE), jnp.float32)
+        out = (
+            jax.ShapeDtypeStruct((clusters, lane_cells.shape[0], TILE), jnp.float32),
+            jax.ShapeDtypeStruct((shards, clusters // shards, TILE), jnp.float32),
+        )
         scratch = []
     else:
         many = 2 if kind == "max" else 1
@@ -131,7 +138,7 @@
         functools.partial(sweep_kernel, kind, math.gcd(sub_ids.shape[0] // 2, 16)),
         out_shape=out,
         in_specs=[smem] * 3 + [vmem] * 4,
-        out_specs=vmem,
+        out_specs=(vmem, vmem) if kind == "map" else vmem,
         scratch_shapes=scratch,
         compiler_params=pltpu.CompilerParams(vmem_limit_bytes=48 * MIB),
         name="sweep_" + kind,
@@ -202,53 +209,113 @@
     )(part, old, logmass)
 
 
-def scatter_kernel(axis, n, moved, out, held, send, recv, own):
+def scatter_kernel(axis, n, ny, num, den, out, first_y, ring_a, ring_b, last_y, held, *sems):
+    nz = n // ny
     me = greet(axis, n)
-    per = moved.shape[0] // n
-    copies = []
+    z, y = me // ny, lax.rem(me, ny)
+    per, features = num.shape[2], num.shape[3]
+    half = per // 4
+    other = ny - 1 - y
+
+    def device(at):
+        return lax.rem(at + nz, nz) * ny + y
+
+    def copy(src, dst, sem, k, peer):
+        made = pltpu.make_async_remote_copy(
+            src_ref=src, dst_ref=dst, send_sem=sems[2 * sem].at[k], recv_sem=sems[2 * sem + 1].at[k],
+            device_id={axis: peer}, device_id_type=MESH)
+        made.start()
+        return made
+
+    partner = z * ny + other
+    sign = (1, -1)
+
+    def block(d, step):
+        return lax.rem(z - sign[d] * (1 + step) + 2 * nz, nz)
+
+    def group(d, base):
+        return pl.ds(base + d * half, half)
+
+    over_y = [[None] * nz for _ in sign]
+    over_a = [[None] * nz for _ in sign]
+    over_b = [[None] * nz for _ in sign]
+    for d in range(2):
+        at = block(d, 0)
+        over_a[d][0] = copy(num.at[at, :, group(d, 0)], ring_a.at[d, 0], 1, d * nz, device(z + sign[d]))
+    for step in range(nz):
+        for d in range(2):
+            at = block(d, step)
+            over_y[d][step] = copy(num.at[at, other, group(d, 2 * half)], first_y.at[d, step], 0, d * nz + step, partner)
+    others = []
     for k in range(1, n):
         peer = lax.rem(me + k, n)
-        copy = pltpu.make_async_remote_copy(
-            src_ref=moved.at[pl.ds(peer * per, per)], dst_ref=held.at[k], send_sem=send.at[k], recv_sem=recv.at[k],
-            device_id={axis: peer}, device_id_type=MESH)
-        copy.start()
-        copies.append(copy)
-    local = pltpu.make_async_copy(moved.at[pl.ds(me * per, per)], held.at[0], own)
-    local.start()
-    local.wait()
-    for copy in copies:
-        copy.wait()
-
-    features = out.shape[0]
-
-    def one(c):
-        total = held[0, c]
-        for k in range(1, n):
-            total = total + held[k, c]
-        weight = total[features:features + 1]
-        weight = jnp.where(weight > 0.0, weight, 1.0)
-        out[:, pl.ds(pl.multiple_of(c * TILE, TILE), TILE)] = total[:features] / weight
-
-    pl.loop(0, per)(one)
-
-
-def scatter(axis, ident, n, features, moved):
-    clusters = moved.shape[0]
-    per = clusters // n
+        others.append(copy(den.at[peer], held.at[k], 4, k, peer))
+    for step in range(nz):
+        at = [block(d, step) for d in range(2)]
+        for d in range(2):
+            over_y[d][step].wait_recv()
+            first_y[d, step] += num[at[d], y, group(d, 2 * half)]
+            if step > 0:
+                over_b[d][step - 1].wait_recv()
+                first_y[d, step] += ring_b[d, step - 1]
+            if step < nz - 1:
+                over_b[d][step] = copy(first_y.at[d, step], ring_b.at[d, step], 2, d * nz + step, device(z + sign[d]))
+            if step > 0:
+                over_a[d][step - 1].wait_recv()
+                ring_a[d, step - 1] += num[at[d], :, group(d, 0)]
+            if 0 < step < nz - 1:
+                over_a[d][step] = copy(ring_a.at[d, step - 1], ring_a.at[d, step], 1, d * nz + step, device(z + sign[d]))
+    over_last = [copy(ring_a.at[d, nz - 2, other], last_y.at[d], 3, d, partner) for d in range(2)]
+    for made in others:
+        made.wait_recv()
+    total = den[me]
+    for k in range(1, n):
+        total = total + held[k]
+    total = jnp.where(total > 0.0, total, 1.0)
+
+    def put(c, value):
+        out[:, c * TILE:(c + 1) * TILE] = value / total[c:c + 1]
+
+    for d in range(2):
+        for c in range(half):
+            put(2 * half + d * half + c, first_y[d, nz - 1, c])
+    for d in range(2):
+        over_last[d].wait_recv()
+        for c in range(half):
+            put(d * half + c, ring_a[d, nz - 2, y, c] + last_y[d, c])
+    for made in others + over_last:
+        made.wait_send()
+    for d in range(2):
+        for step in range(nz):
+            over_y[d][step].wait_send()
+        for step in range(nz - 1):
+            over_a[d][step].wait_send()
+            over_b[d][step].wait_send()
+
+
+def scatter(axis, ident, n, ny, num, den):
+    clusters, features, width = num.shape
+    per, nz = clusters // n, n // ny
+    quarter = per // 4
+    vmem = pl.BlockSpec(memory_space=pltpu.VMEM)
+    sems = []
+    for many in (2 * nz, 2 * nz, 2 * nz, 2, n):
+        sems += [pltpu.SemaphoreType.DMA((many,))] * 2
     return pl.pallas_call(
-        functools.partial(scatter_kernel, axis, n),
-        out_shape=jax.ShapeDtypeStruct((features, per * TILE), jnp.float32),
-        in_specs=[pl.BlockSpec(memory_space=pl.ANY)],
-        out_specs=pl.BlockSpec(memory_space=pltpu.VMEM),
+        functools.partial(scatter_kernel, axis, n, ny),
+        out_shape=jax.ShapeDtypeStruct((features, per * width), jnp.float32),
+        in_specs=[vmem, vmem],
+        out_specs=vmem,
         scratch_shapes=[
-            pltpu.VMEM((n, per) + moved.shape[1:], jnp.float32),
-            pltpu.SemaphoreType.DMA((n,)),
-            pltpu.SemaphoreType.DMA((n,)),
-            pltpu.SemaphoreType.DMA,
-        ],
-        compiler_params=pltpu.CompilerParams(collective_id=ident, has_side_effects=True, vmem_limit_bytes=48 * MIB),
+            pltpu.VMEM((2, nz, quarter, features, width), jnp.float32),
+            pltpu.VMEM((2, nz - 1, ny, quarter, features, width), jnp.float32),
+            pltpu.VMEM((2, nz - 1, quarter, features, width), jnp.float32),
+            pltpu.VMEM((2, quarter, features, width), jnp.float32),
+            pltpu.VMEM((n, per, width), jnp.float32),
+        ] + sems,
+        compiler_params=pltpu.CompilerParams(collective_id=ident, has_side_effects=True, vmem_limit_bytes=32 * MIB),
         name="scatter",
-    )(moved)
+    )(num.reshape(nz, ny, per, features, width), den)
 
 
 def pair_table(pair_lists, tgt_block, per_block, capacity):
@@ -275,7 +342,6 @@
 
 
 def shards(source_cells, target_cells, source_mass, target_mass, source_count, target_count, pair_lists):
-    features = source_cells.shape[0]
     n_src, n_tgt = lax.axis_size("src"), lax.axis_size("tgt")
     capacity = 2 * pair_lists.size // n_tgt
     own_src, own_tgt, own = pair_table(pair_lists, lax.axis_index("tgt"), target_count.shape[0], capacity)
@@ -289,8 +355,8 @@
         u = reduce(kind, "tgt", 2 * step, part, u, src_logmass)
         part = sweep(kind, n_src, own_src, own_tgt, own, source_cells, target_cells, u, v)
         v = reduce(kind, "src", 2 * step + 1, part, v, tgt_logmass)
-    moved = sweep("map", n_tgt, own_tgt, own_src, own, target_cells, source_cells, v, u)
-    mapped = scatter("tgt", 2 * ITERS, n_tgt, features, moved)
+    num, den = sweep("map", n_tgt, own_tgt, own_src, own, target_cells, source_cells, v, u)
+    mapped = scatter("tgt", 2 * ITERS, n_tgt, 2, num, den)
     source_pot = jnp.where(src_live, 0.5 * u + src_norm, 0.0)
     target_pot = jnp.where(tgt_live, 0.5 * v + tgt_norm, 0.0)
     return source_pot.reshape(-1), target_pot.reshape(-1), mapped

time: 259 us -> 183 us (0.71)
  Pallas kernels: 242 us -> 165 us
    pallas_call x1, Pallas kernels: 129 us -> 53.6 us  [scatter(): pl.pallas_call(functools.partial(scatter_kernel, axis, n, ny), out_shape=...]
where the time goes in v3:
time: 183 us; the launch traced here: 180 us
  Pallas kernels  165 us (90%)
  other arithmetic  7.68 us (4%)
  local copies, waits for them, and re-layouts  5.86 us (3%)
    pallas_call x4, Pallas kernels, reduce(): pl.pallas_call(functools.partial(reduce_kernel, kind, axis, n), out_shape...  76.4 us
    pallas_call x1, Pallas kernels, scatter(): pl.pallas_call(functools.partial(scatter_kernel, axis, n, ny), out_shape=...  53.6 us
    pallas_call x5, Pallas kernels, sweep(): pl.pallas_call(functools.partial(sweep_kernel, kind, math.gcd(sub_ids.sha...  35.3 us
    reduce_sum x2, other arithmetic, side(): norm = jnp.sum(wide * wide, axis=0).reshape(2 * clusters, 128)  4.56 us
    unnamed x12, local copies, waits for them, and re-layouts  3.7 us

profile of v3, /device:TPU:24, one launch (start us, length us, event | category | flops | bytes accessed | tf_op | source)
XLA Modules:
  0.0 179.7 jit_solution(15312848922006143593)
XLA Ops:
  0.6 0.0 copy-start
  0.6 0.0 copy-start.3
  0.7 0.0 copy-start.4
  0.7 1.5 convert_reduce_fusion
  2.2 0.1 iota_add_fusion
  2.2 0.8 copy.13
  3.0 0.1 reshape.169
  3.1 0.1 reshape.167
  3.2 0.3 reduce-window.9
  3.5 0.1 slice.7
  3.6 0.1 slice_reduce_fusion
  3.7 0.1 add_bitcast_fusion
  3.8 0.2 select_reduce_fusion
  4.0 0.7 lt.48
  4.8 0.1 lt.49
  4.9 0.7 lt.53
  5.7 0.1 lt.54
  5.8 0.0 copy-start.1
  5.9 2.3 %multiply_reduce_fusion = f32[32768]{0:T(1024)S(1)} fusion(bf16[32,32768]{1,0:T(8,128)(2,1)} %lane_cells.9), kind=kLoop, calls=%fused_computation | loop fusion | flops 3112960 | bytes 2228224 | tf_op jit(solution)/shard_map/reduce_sum | solution.py:337
  8.2 2.2 %multiply_reduce_fusion.1 = f32[32768]{0:T(1024)S(1)} fusion(bf16[32,32768]{1,0:T(8,128)(2,1)} %sub_cells.9), kind=kLoop, calls=%fused_computation.1 | loop fusion | flops 3112960 | bytes 2228224 | tf_op jit(solution)/shard_map/reduce_sum | solution.py:337
  10.4 0.0 copy-done.3
  10.5 0.0 copy-done.4
  10.5 0.1 bitcast_select_fusion
  10.6 0.0 copy-done
  10.7 0.0 copy-done.1
  10.7 7.5 %sweep_max.2.part = f32[16,16,128]{2,1,0:T(8,128)S(1)} custom-call(s32[128]{0:T(128)S(1)} %get-tuple-element.8.sub_ids.lane_ids, s32[128]{0:T(128)S(1)} %get-tuple-element.7.lane_ids.sub_ids, s32[1]{0:T(128)} %bitcast.2.count, bf16[32,32768]{1,0:T(8,128)(2,1)S(1)} %copy-done.1, bf16[32,32768]{1,0:T(8,128)(2,1)S(1)} %copy-done, ...), custom_call_target="tpu_custom_call" | custom-call | tf_op jit(solution)/shard_map/sweep_max/pallas_call | solution.py:137
  18.1 25.2 %reduce_max_tgt.1.sub_pot.lane_pot.old = f32[256,128]{1,0:T(8,128)S(1)} custom-call(f32[16,16,128]{2,1,0:T(8,128)S(1)} %sweep_max.2.part, f32[256,128]{1,0:T(8,128)S(1)} %bitcast_multiply_fusion.lane_pot.old, f32[256,128]{1,0:T(8,128)S(1)} %get-tuple-element.13.logmass), custom_call_target="tpu_custom_call" | custom-call | tf_op jit(solution)/shard_map/reduce_max_tgt/pallas_call | solution.py:201
  43.3 7.4 %sweep_max.3.part = f32[16,16,128]{2,1,0:T(8,128)S(1)} custom-call(s32[128]{0:T(128)S(1)} %get-tuple-element.7.lane_ids.sub_ids, s32[128]{0:T(128)S(1)} %get-tuple-element.8.sub_ids.lane_ids, s32[1]{0:T(128)} %bitcast.2.count, bf16[32,32768]{1,0:T(8,128)(2,1)S(1)} %copy-done, bf16[32,32768]{1,0:T(8,128)(2,1)S(1)} %copy-done.1, ...), custom_call_target="tpu_custom_call" | custom-call | tf_op jit(solution)/shard_map/sweep_max/pallas_call | solution.py:137
  50.7 14.6 %reduce_max_src.1.sub_pot.lane_pot.old = f32[256,128]{1,0:T(8,128)S(1)} custom-call(f32[16,16,128]{2,1,0:T(8,128)S(1)} %sweep_max.3.part, f32[256,128]{1,0:T(8,128)S(1)} %fusion.3.sub_pot.lane_pot.old, f32[256,128]{1,0:T(8,128)S(1)} %get-tuple-element.9.logmass), custom_call_target="tpu_custom_call" | custom-call | tf_op jit(solution)/shard_map/reduce_max_src/pallas_call | solution.py:201
  65.3 5.5 %sweep_sum.2.part = f32[16,16,128]{2,1,0:T(8,128)S(1)} custom-call(s32[128]{0:T(128)S(1)} %get-tuple-element.8.sub_ids.lane_ids, s32[128]{0:T(128)S(1)} %get-tuple-element.7.lane_ids.sub_ids, s32[1]{0:T(128)} %bitcast.2.count, bf16[32,32768]{1,0:T(8,128)(2,1)S(1)} %copy-done.1, bf16[32,32768]{1,0:T(8,128)(2,1)S(1)} %copy-done, ...), custom_call_target="tpu_custom_call" | custom-call | tf_op jit(solution)/shard_map/sweep_sum/pallas_call | solution.py:137
  70.8 20.6 %reduce_sum_tgt.1.sub_pot.lane_pot = f32[256,128]{1,0:T(8,128)S(1)} custom-call(f32[16,16,128]{2,1,0:T(8,128)S(1)} %sweep_sum.2.part, f32[256,128]{1,0:T(8,128)S(1)} %reduce_max_tgt.1.sub_pot.lane_pot.old, f32[256,128]{1,0:T(8,128)S(1)} %get-tuple-element.13.logmass), custom_call_target="tpu_custom_call" | custom-call | tf_op jit(solution)/shard_map/reduce_sum_tgt/pallas_call | solution.py:201
  91.4 5.4 %sweep_sum.3.part = f32[16,16,128]{2,1,0:T(8,128)S(1)} custom-call(s32[128]{0:T(128)S(1)} %get-tuple-element.7.lane_ids.sub_ids, s32[128]{0:T(128)S(1)} %get-tuple-element.8.sub_ids.lane_ids, s32[1]{0:T(128)} %bitcast.2.count, bf16[32,32768]{1,0:T(8,128)(2,1)S(1)} %copy-done, bf16[32,32768]{1,0:T(8,128)(2,1)S(1)} %copy-done.1, ...), custom_call_target="tpu_custom_call" | custom-call | tf_op jit(solution)/shard_map/sweep_sum/pallas_call | solution.py:137
  96.9 16.0 %reduce_sum_src.1.sub_pot = f32[256,128]{1,0:T(8,128)S(1)} custom-call(f32[16,16,128]{2,1,0:T(8,128)S(1)} %sweep_sum.3.part, f32[256,128]{1,0:T(8,128)S(1)} %reduce_max_src.1.sub_pot.lane_pot.old, f32[256,128]{1,0:T(8,128)S(1)} %get-tuple-element.9.logmass), custom_call_target="tpu_custom_call" | custom-call | tf_op jit(solution)/shard_map/reduce_sum_src/pallas_call | solution.py:201
  112.9 0.7 fusion.2
  113.6 9.5 %sweep_map.1 = (f32[128,32,256]{2,1,0:T(8,128)}, f32[16,8,256]{2,1,0:T(8,128)S(1)}) custom-call(s32[128]{0:T(128)S(1)} %get-tuple-element.8.sub_ids.lane_ids, s32[128]{0:T(128)S(1)} %get-tuple-element.7.lane_ids.sub_ids, s32[1]{0:T(128)} %bitcast.2.count, bf16[32,32768]{1,0:T(8,128)(2,1)S(1)} %copy-done.1, bf16[32,32768]{1,0:T(8,128)(2,1)S(1)} %copy-done, ...), custom_call_target="tpu_custom_call" | custom-call | tf_op jit(solution)/shard_map/sweep_map/pallas_call | solution.py:137
  123.1 0.0 copy-start.2
  123.1 2.2 %copy-done.2 = f32[128,32,256]{2,1,0:T(8,128)S(1)} copy-done((f32[128,32,256]{2,1,0:T(8,128)S(1)}, f32[128,32,256]{2,1,0:T(8,128)}, u32[]{:S(2)}) %copy-start.2) | copy-done | bytes 4194328
  125.3 53.6 %scatter.1 = f32[32,2048]{1,0:T(8,128)S(1)} custom-call(f32[8,2,8,32,256]{4,3,2,1,0:T(8,128)S(1)} %bitcast.29, f32[16,8,256]{2,1,0:T(8,128)S(1)} %get-tuple-element.6.den), custom_call_target="tpu_custom_call" | custom-call | tf_op jit(solution)/shard_map/scatter/pallas_call | solution.py:304
  178.9 0.7 copy.16
  (9 shorter events, 0.1 us)
Async XLA Ops:
  0.6 10.0 %copy-start = (bf16[32,32768]{1,0:T(8,128)(2,1)S(1)}, bf16[32,32768]{1,0:T(8,128)(2,1)}, u32[]{:S(2)}) copy-start(bf16[32,32768]{1,0:T(8,128)(2,1)} %lane_cells.9) | copy-start | bytes 6291460
  0.6 9.8 %copy-start.3 = (f32[32768]{0:T(1024)S(1)}, f32[32768]{0:T(1024)}, u32[]{:S(2)}) copy-start(f32[32768]{0:T(1024)} %param.10) | copy-start | bytes 393220
  0.7 9.8 %copy-start.4 = (f32[32768]{0:T(1024)S(1)}, f32[32768]{0:T(1024)}, u32[]{:S(2)}) copy-start(f32[32768]{0:T(1024)} %param.9) | copy-start | bytes 393220
  5.8 4.8 %copy-start.1 = (bf16[32,32768]{1,0:T(8,128)(2,1)S(1)}, bf16[32,32768]{1,0:T(8,128)(2,1)}, u32[]{:S(2)}) copy-start(bf16[32,32768]{1,0:T(8,128)(2,1)} %sub_cells.9) | copy-start | bytes 6291460
  123.1 2.2 %copy-start.2 = (f32[128,32,256]{2,1,0:T(8,128)S(1)}, f32[128,32,256]{2,1,0:T(8,128)}, u32[]{:S(2)}) copy-start(f32[128,32,256]{2,1,0:T(8,128)} %get-tuple-element.5) | copy-start | bytes 12582916

commit v4 on v1

v4 whole, which is shorter than its diff:
```python
import functools
import math

import jax
import jax.numpy as jnp
from jax import lax
from jax.experimental import pallas as pl
from jax.experimental.pallas import tpu as pltpu
from jax.sharding import PartitionSpec as P

MESH = pl.DeviceIdType.MESH
EMPTY = -1e30
TILE = 256
SUB = 8
AUX = 16
NY = 2
MIB = 1 << 20
ROW_SUB, ROW_LANE, ROW_KEEP, ROW_LAST, COL_SUB, COL_LANE, COL_KEEP, COL_LAST = range(8)


def split3(row):
    high = row.astype(jnp.bfloat16).astype(jnp.float32)
    rest = row - high
    mid = rest.astype(jnp.bfloat16).astype(jnp.float32)
    low = rest - mid
    return high, mid, low


def cluster_row(ref, cluster):
    first = ref[pl.ds(2 * cluster, 1), :]
    second = ref[pl.ds(2 * cluster + 1, 1), :]
    return jnp.concatenate([first, second], axis=1)


def aux_rows(row, offset, other):
    at = lax.broadcasted_iota(jnp.int32, (AUX, TILE), 0)
    high, mid, low = split3(row)
    out = jnp.where((at >= other) & (at < other + 3), 1.0, 0.0)
    out = jnp.where(at == offset, high, out)
    out = jnp.where(at == offset + 1, mid, out)
    out = jnp.where(at == offset + 2, low, out)
    return out.astype(jnp.bfloat16)


def kernel(
    sizes, table, x_cells, y_cells, u0, v0, x_mass, y_mass, u_out, v_out, out,
    xs, ys, u1, v1, parts, helds, slot_m, slot_s, slot_n, slot_d, send_a, send_y, den, held_d,
    first_y, ring_a, ring_b, last_y, *sems,
):
    n_src, n_tgt, slots = sizes
    step = math.gcd(slots, 16)
    features = x_cells.shape[0]
    me_src, me_tgt = lax.axis_index("src"), lax.axis_index("tgt")
    barrier = pltpu.get_barrier_semaphore()
    for axis, me, n in (("tgt", me_tgt, n_tgt), ("src", me_src, n_src)):
        for k in range(1, n):
            pl.semaphore_signal(barrier, inc=1, device_id={axis: lax.rem(me + k, n)}, device_id_type=MESH)

    slot_m[slots] = jnp.full((SUB, TILE), EMPTY, jnp.float32)
    slot_s[slots] = jnp.zeros((SUB, TILE), jnp.float32)
    slot_n[slots] = jnp.zeros((features, TILE), jnp.float32)
    slot_d[pl.ds(slots, SUB), :] = jnp.zeros((SUB, TILE), jnp.float32)

    def entry(which, p):
        return table[which * slots + p]

    def sweep(kind, first, sub_cells, lane_cells, sub_pot, lane_pot):
        def tile(p, carry):
            a, b, keep = entry(first, p), entry(first + 1, p), entry(first + 2, p)
            sub, lane = sub_cells[a], lane_cells[b]
            left = jnp.concatenate([sub, aux_rows(cluster_row(sub_pot, a), 0, 3)], axis=0)
            right = jnp.concatenate([lane, aux_rows(cluster_row(lane_pot, b), 3, 0)], axis=0)
            score = lax.dot_general(left, right, (((0,), (0,)), ((), ())), preferred_element_type=jnp.float32)
            hold = keep.astype(jnp.float32)
            if kind == "max":
                score = score.reshape(TILE // SUB, SUB, TILE)
                best = jnp.max(score, axis=0)
                part = jnp.sum(jnp.exp(score - best[None]), axis=0)
                old = carry[0] * hold + (1.0 - hold) * EMPTY
                new = jnp.maximum(old, best)
                total = carry[1] * hold * jnp.exp(old - new) + part * jnp.exp(best - new)
                slot_m[p] = new
                slot_s[p] = total
                return new, total
            weight = jnp.exp(score)
            if kind == "sum":
                total = carry[0] * hold + jnp.sum(weight.reshape(TILE // SUB, SUB, TILE), axis=0)
                slot_s[p] = total
                return (total,)
            high = weight.astype(jnp.bfloat16)
            low = (weight - high.astype(jnp.float32)).astype(jnp.bfloat16)
            ones = jnp.where(lax.broadcasted_iota(jnp.int32, (AUX, TILE), 0) == 0, 1.0, 0.0).astype(jnp.bfloat16)
            cells = jnp.concatenate([sub, ones], axis=0)
            moved = jnp.dot(cells, high, preferred_element_type=jnp.float32)
            moved = moved + jnp.dot(cells, low, preferred_element_type=jnp.float32)
            total = carry[0] * hold + moved[:features]
            weights = carry[1] * hold + moved[features:features + 1]
            slot_n[p] = total
            slot_d[pl.ds(p, 1), :] = weights
            return total, weights

        def group(g, carry):
            for r in range(step):
                carry = tile(g * step + r, carry)
            return carry

        empty = jnp.zeros((SUB, TILE), jnp.float32)
        if kind == "max":
            start = (empty + EMPTY, empty)
        elif kind == "sum":
            start = (empty,)
        else:
            start = (jnp.zeros((features, TILE), jnp.float32), jnp.zeros((1, TILE), jnp.float32))
        lax.fori_loop(0, slots // step, group, start)

    def reduce(kind, which, axis, me, n, last, old, mass, new):
        part, held = parts.at[which], helds.at[which]
        rows = old.shape[0] // n
        per = rows // 2

        def finish(c):
            at = entry(last, c)
            if kind == "max":
                best = jnp.max(slot_m[at], axis=0, keepdims=True)
                row = jnp.sum(slot_s[at] * jnp.exp(slot_m[at] - best), axis=0, keepdims=True)
                value = best + jnp.log(jnp.where(row > 0.0, row, 1.0))
            else:
                value = jnp.sum(slot_s[at], axis=0, keepdims=True)
            part[pl.ds(2 * c, 1), :] = value[:, :128]
            part[pl.ds(2 * c + 1, 1), :] = value[:, 128:]

        def finish_group(g):
            for r in range(per):
                finish(g * per + r)

        pl.loop(0, n)(finish_group)
        if which == 0:
            pl.semaphore_wait(barrier, n_src + n_tgt - 2)
        mine = pl.ds(pl.multiple_of(me * rows, rows), rows)

        def share(src_ref, dst_ref, phase):
            made = []
            for k in range(1, n):
                peer = lax.rem(me + k, n)
                copy = pltpu.make_async_remote_copy(
                    src_ref=src_ref(peer), dst_ref=dst_ref(k),
                    send_sem=sems[2 * phase].at[which, k], recv_sem=sems[2 * phase + 1].at[which, k],
                    device_id={axis: peer}, device_id_type=MESH)
                copy.start()
                made.append(copy)
            return made

        made = share(lambda peer: part.at[pl.ds(pl.multiple_of(peer * rows, rows), rows)],
                     lambda k: held.at[pl.ds(k * rows, rows)], 0)
        for copy in made:
            copy.wait_recv()
        own = part[mine, :]
        if kind == "max":
            best = own
            for k in range(1, n):
                best = jnp.maximum(best, held[k * rows:(k + 1) * rows])
            total = jnp.exp(own - best)
            for k in range(1, n):
                total = total + jnp.exp(held[k * rows:(k + 1) * rows] - best)
            lse = best + jnp.log(total)
        else:
            total = own
            for k in range(1, n):
                total = total + held[k * rows:(k + 1) * rows]
            lse = jnp.log(jnp.where(total > 0.0, total, 1.0))
        logmass = mass[mine, :]
        new[mine, :] = jnp.where(logmass > 0.5 * EMPTY, old[mine, :] + logmass - lse, EMPTY)
        sent = share(lambda peer: new.at[mine], lambda k: new.at[mine], 1)
        for copy in made:
            copy.wait_send()
        for copy in sent:
            copy.wait()

    def arrange(c):
        lanes = pl.ds(pl.multiple_of(c * TILE, TILE), TILE)
        xs[c] = x_cells[:, lanes] * jnp.bfloat16(4.0)
        ys[c] = y_cells[:, lanes]

    pl.loop(0, x_cells.shape[1] // TILE)(arrange)
    sweep("max", ROW_SUB, ys, xs, v0, u0)
    reduce("max", 0, "tgt", me_tgt, n_tgt, ROW_LAST, u0, x_mass, u1)
    sweep("max", COL_SUB, xs, ys, u1, v0)
    reduce("max", 1, "src", me_src, n_src, COL_LAST, v0, y_mass, v1)
    sweep("sum", ROW_SUB, ys, xs, v1, u1)
    reduce("sum", 2, "tgt", me_tgt, n_tgt, ROW_LAST, u1, x_mass, u_out)
    sweep("sum", COL_SUB, xs, ys, u_out, v1)
    reduce("sum", 3, "src", me_src, n_src, COL_LAST, v1, y_mass, v_out)
    sweep("map", ROW_SUB, ys, xs, v_out, u_out)

    n, nz = n_tgt, n_tgt // NY
    z, y = me_tgt // NY, lax.rem(me_tgt, NY)
    other = NY - 1 - y
    per = out.shape[1] // TILE
    half = per // 4
    sign = (1, -1)

    def device(at):
        return lax.rem(at + nz, nz) * NY + y

    def block(d, hop):
        return lax.rem(z - sign[d] * (1 + hop) + 2 * nz, nz)

    def own(at, side, base, c):
        return slot_n[entry(ROW_LAST, (at * NY + side) * per + base + c)]

    def copy(src, dst, sem, k, peer):
        made = pltpu.make_async_remote_copy(
            src_ref=src, dst_ref=dst, send_sem=sems[2 * sem].at[k], recv_sem=sems[2 * sem + 1].at[k],
            device_id={"tgt": peer}, device_id_type=MESH)
        made.start()
        return made

    partner = z * NY + other
    over_y = [[None] * nz for _ in sign]
    over_a = [[None] * nz for _ in sign]
    over_b = [[None] * nz for _ in sign]
    for d in range(2):
        for side in range(NY):
            for c in range(half):
                send_a[d, side, c] = own(block(d, 0), side, d * half, c)
        over_a[d][0] = copy(send_a.at[d], ring_a.at[d, 0], 3, d * nz, device(z + sign[d]))
    for hop in range(nz):
        for d in range(2):
            for c in range(half):
                send_y[d, hop, c] = own(block(d, hop), other, (2 + d) * half, c)
            over_y[d][hop] = copy(send_y.at[d, hop], first_y.at[d, hop], 2, d * nz + hop, partner)

    def gather(t):
        for c in range(per):
            den[t, pl.ds(c, 1), :] = slot_d[pl.ds(entry(ROW_LAST, t * per + c), 1), :]

    pl.loop(0, n)(gather)
    others = []
    for k in range(1, n):
        peer = lax.rem(me_tgt + k, n)
        others.append(copy(den.at[peer], held_d.at[k], 6, k, peer))
    for hop in range(nz):
        at = [block(d, hop) for d in range(2)]
        for d in range(2):
            over_y[d][hop].wait_recv()
            if hop > 0:
                over_b[d][hop - 1].wait_recv()
            for c in range(half):
                value = first_y[d, hop, c] + own(at[d], y, (2 + d) * half, c)
                if hop > 0:
                    value = value + ring_b[d, hop - 1, c]
                first_y[d, hop, c] = value
            if hop < nz - 1:
                over_b[d][hop] = copy(first_y.at[d, hop], ring_b.at[d, hop], 4, d * nz + hop, device(z + sign[d]))
            if hop > 0:
                over_a[d][hop - 1].wait_recv()
                for side in range(NY):
                    for c in range(half):
                        ring_a[d, hop - 1, side, c] += own(at[d], side, d * half, c)
            if 0 < hop < nz - 1:
                over_a[d][hop] = copy(ring_a.at[d, hop - 1], ring_a.at[d, hop], 3, d * nz + hop, device(z + sign[d]))
    over_last = [copy(ring_a.at[d, nz - 2, other], last_y.at[d], 5, d, partner) for d in range(2)]
    for made in others:
        made.wait_recv()
    total = den[me_tgt]
    for k in range(1, n):
        total = total + held_d[k]
    total = jnp.where(total > 0.0, total, 1.0)

    def put(c, value):
        out[:, c * TILE:(c + 1) * TILE] = value / total[c:c + 1]

    for d in range(2):
        for c in range(half):
            put((2 + d) * half + c, first_y[d, nz - 1, c])
    for d in range(2):
        over_last[d].wait_recv()
        for c in range(half):
            put(d * half + c, ring_a[d, nz - 2, y, c] + last_y[d, c])
    for made in others + over_last:
        made.wait_send()
    for d in range(2):
        for hop in range(nz):
            over_y[d][hop].wait_send()
        for hop in range(nz - 1):
            over_a[d][hop].wait_send()
            over_b[d][hop].wait_send()


def transport(n_src, n_tgt, slots, table, x_cells, y_cells, u0, v0, x_mass, y_mass):
    features = x_cells.shape[0]
    clusters = x_cells.shape[1] // TILE
    per, nz = clusters // n_tgt, n_tgt // NY
    quarter = per // 4
    f32 = jnp.float32
    vmem = pl.BlockSpec(memory_space=pltpu.VMEM)
    dma = pltpu.SemaphoreType.DMA
    most = max(n_src, n_tgt)
    sems = [dma((4, most))] * 4
    for many in (2 * nz, 2 * nz, 2 * nz, 2, n_tgt):
        sems += [dma((many,))] * 2
    scratch = [
        pltpu.VMEM((clusters, features, TILE), jnp.bfloat16),
        pltpu.VMEM((clusters, features, TILE), jnp.bfloat16),
        pltpu.VMEM(u0.shape, f32),
        pltpu.VMEM(v0.shape, f32),
        pltpu.VMEM((4,) + u0.shape, f32),
        pltpu.VMEM((4,) + u0.shape, f32),
        pltpu.VMEM((slots + 1, SUB, TILE), f32),
        pltpu.VMEM((slots + 1, SUB, TILE), f32),
        pltpu.VMEM((slots + 1, features, TILE), f32),
        pltpu.VMEM((slots + SUB, TILE), f32),
        pltpu.VMEM((2, NY, quarter, features, TILE), f32),
        pltpu.VMEM((2, nz, quarter, features, TILE), f32),
        pltpu.VMEM((n_tgt, per, TILE), f32),
        pltpu.VMEM((n_tgt, per, TILE), f32),
        pltpu.VMEM((2, nz, quarter, features, TILE), f32),
        pltpu.VMEM((2, nz - 1, NY, quarter, features, TILE), f32),
        pltpu.VMEM((2, nz - 1, quarter, features, TILE), f32),
        pltpu.VMEM((2, quarter, features, TILE), f32),
    ]
    return pl.pallas_call(
        functools.partial(kernel, (n_src, n_tgt, slots)),
        out_shape=(
            jax.ShapeDtypeStruct(u0.shape, f32),
            jax.ShapeDtypeStruct(v0.shape, f32),
            jax.ShapeDtypeStruct((features, per * TILE), f32),
        ),
        in_specs=[pl.BlockSpec(memory_space=pltpu.SMEM)] + [vmem] * 6,
        out_specs=(vmem, vmem, vmem),
        scratch_shapes=scratch + sems,
        compiler_params=pltpu.CompilerParams(collective_id=0, has_side_effects=True, vmem_limit_bytes=40 * MIB),
        name="transport",
    )(table, x_cells, y_cells, u0, v0, x_mass, y_mass)


def pair_tables(pair_lists, tgt_block, per_block, slots):
    width = pair_lists.shape[1]
    flat = pair_lists.reshape(-1)
    chosen = flat // per_block == tgt_block
    targets = flat % per_block
    sources = jnp.arange(flat.shape[0], dtype=jnp.int32) // width
    places = jnp.arange(slots, dtype=jnp.int32)
    rank = jnp.cumsum(chosen.astype(jnp.int32)) - 1
    matches = (rank[None, :] == places[:, None]) & chosen[None, :]
    row_src = jnp.sum(jnp.where(matches, sources[None, :], 0), axis=1)
    row_tgt = jnp.sum(jnp.where(matches, targets[None, :], 0), axis=1)
    live = places < jnp.sum(chosen.astype(jnp.int32))
    before = (row_tgt[None, :] < row_tgt[:, None]) | (
        (row_tgt[None, :] == row_tgt[:, None]) & (places[None, :] < places[:, None]))
    order = jnp.where(live, jnp.sum((before & live[None, :]).astype(jnp.int32), axis=1), places)
    moves = order[None, :] == places[:, None]
    col_src = jnp.sum(jnp.where(moves, row_src[None, :], 0), axis=1)
    col_tgt = jnp.sum(jnp.where(moves, row_tgt[None, :], 0), axis=1)

    def ends(kept):
        same = jnp.concatenate([jnp.zeros((1,), jnp.int32), (kept[1:] == kept[:-1]).astype(jnp.int32)])
        found = (kept[None, :] == places[:, None]) & live[None, :]
        last = jnp.max(jnp.where(found, places[None, :], -1), axis=1)
        return same, jnp.where(last < 0, slots, last)

    row_keep, row_last = ends(row_src)
    col_keep, col_last = ends(col_tgt)
    return jnp.concatenate([row_tgt, row_src, row_keep, row_last, col_src, col_tgt, col_keep, col_last])


def side(cells, mass, count):
    clusters = count.shape[0]
    wide = cells.astype(jnp.float32)
    norm = jnp.sum(wide * wide, axis=0).reshape(2 * clusters, 128)
    place = jnp.arange(2, dtype=jnp.int32)[None, :, None] * 128 + jnp.arange(128, dtype=jnp.int32)[None, None, :]
    live = (place < count[:, None, None]).reshape(2 * clusters, 128)
    logmass = jnp.where(live, jnp.log(mass).reshape(2 * clusters, 128), EMPTY)
    return norm, live, logmass


def shards(source_cells, target_cells, source_mass, target_mass, source_count, target_count, pair_lists):
    n_src, n_tgt = lax.axis_size("src"), lax.axis_size("tgt")
    slots = 2 * pair_lists.size // n_tgt
    table = pair_tables(pair_lists, lax.axis_index("tgt"), target_count.shape[0], slots)
    src_norm, src_live, src_logmass = side(source_cells, source_mass, source_count)
    tgt_norm, tgt_live, tgt_logmass = side(target_cells, target_mass, target_count)
    u0 = -2.0 * src_norm
    v0 = jnp.where(tgt_live, -2.0 * tgt_norm, EMPTY)
    u, v, mapped = transport(
        n_src, n_tgt, slots, table, source_cells, target_cells, u0, v0, src_logmass, tgt_logmass)
    source_pot = jnp.where(src_live, 0.5 * u + src_norm, 0.0)
    target_pot = jnp.where(tgt_live, 0.5 * v + tgt_norm, 0.0)
    return source_pot.reshape(-1), target_pot.reshape(-1), mapped


def solution(mesh):
    return jax.shard_map(
        shards,
        mesh=mesh,
        in_specs=(P(None, "src"), P(None, "tgt"), P("src"), P("tgt"), P("src"), P("tgt"), P("src", None)),
        out_specs=(P("src"), P("tgt"), P(None, ("src", "tgt"))),
        check_vma=False,
    )
```

time: 402 us -> 165 us (0.41); the launches traced: 395 us -> 164 us
  Pallas kernels: 381 us -> 151 us
    pallas_call x10 -> x1, Pallas kernels: 381 us -> 151 us  [transport(): pl.pallas_call(functools.partial(kernel, (n_src, n_tgt, slots)), out_shap...]
where the time goes in v4:
time: 165 us; the launch traced here: 164 us
  Pallas kernels  151 us (92%)
  other arithmetic  7.88 us (5%)
  local copies, waits for them, and re-layouts  4.5 us (3%)
    pallas_call x1, Pallas kernels, transport(): pl.pallas_call(functools.partial(kernel, (n_src, n_tgt, slots)), out_shap...  151 us

profile of v4, /device:TPU:24, one launch (start us, length us, event | category | flops | bytes accessed | tf_op | source)
XLA Modules:
  0.0 164.4 jit_solution(6745605307594524338)
XLA Ops:
  0.6 0.0 copy-start
  0.6 1.5 convert_reduce_fusion.1
  2.1 0.6 iota_compare_fusion.5
  2.8 0.1 iota_add_fusion
  2.9 0.8 copy.13
  3.7 0.1 reshape.178
  3.7 0.1 reshape.176
  3.9 0.3 reduce-window.9
  4.2 0.1 slice.19
  4.3 0.1 slice_reduce_fusion
  4.4 0.1 add_bitcast_fusion
  4.5 0.2 select_reduce_fusion
  4.7 0.1 compare_convert_fusion.1
  4.8 0.2 convert_reduce_fusion
  4.9 0.7 iota_select_fusion
  5.6 0.1 select_reduce_fusion.3
  5.7 0.1 compare_convert_fusion
  5.8 0.2 select_reduce_fusion.2
  6.0 0.1 concatenate.3.table
  6.0 0.7 lt.89
  6.8 0.1 lt.90
  6.9 0.7 lt.102
  7.7 0.1 lt.103
  7.8 0.0 copy-start.2
  7.9 0.0 copy-start.3
  7.9 2.3 %multiply_reduce_fusion.1 = f32[32768]{0:T(1024)S(1)} fusion(bf16[32,32768]{1,0:T(8,128)(2,1)} %x_cells.1), kind=kLoop, calls=%fused_computation.1 | loop fusion | flops 3112960 | bytes 2228224 | tf_op jit(solution)/shard_map/reduce_sum | solution.py:370
  10.1 0.0 copy-done
  10.1 0.0 copy-start.1
  10.2 0.6 multiply_reduce_fusion
  10.8 0.0 copy-done.2
  10.8 0.0 copy-done.3
  10.8 0.1 bitcast_select_fusion
  11.0 0.8 copy-done.1
  11.7 151.2 %transport.1 = (f32[256,128]{1,0:T(8,128)S(1)}, f32[256,128]{1,0:T(8,128)S(1)}, f32[32,2048]{1,0:T(8,128)S(1)}) custom-call(s32[1024]{0:T(1024)S(1)} %concatenate.3.table, bf16[32,32768]{1,0:T(8,128)(2,1)S(1)} %copy-done.1, bf16[32,32768]{1,0:T(8,128)(2,1)S(1)} %copy-done, f32[256,128]{1,0:T(8,128)S(1)} %bitcast_multiply_fusion.1.u0, ...), custom_call_target="tpu_custom_call" | custom-call | tf_op jit(solution)/shard_map/transport/pallas_call | solution.py:322
  162.9 0.7 fusion.3
  163.7 0.7 copy.16
  (11 shorter events, 0.1 us)
Async XLA Ops:
  0.6 9.5 %copy-start = (bf16[32,32768]{1,0:T(8,128)(2,1)S(1)}, bf16[32,32768]{1,0:T(8,128)(2,1)}, u32[]{:S(2)}) copy-start(bf16[32,32768]{1,0:T(8,128)(2,1)} %y_cells.1) | copy-start | bytes 6291460
  7.8 2.9 %copy-start.2 = (f32[32768]{0:T(1024)S(1)}, f32[32768]{0:T(1024)}, u32[]{:S(2)}) copy-start(f32[32768]{0:T(1024)} %param.10) | copy-start | bytes 393220
  7.9 2.9 %copy-start.3 = (f32[32768]{0:T(1024)S(1)}, f32[32768]{0:T(1024)}, u32[]{:S(2)}) copy-start(f32[32768]{0:T(1024)} %param.9) | copy-start | bytes 393220
  10.1 1.6 copy-start.1

commit v5 on v4

--- a/solution.py
+++ b/solution.py
@@ -13,6 +13,7 @@
 TILE = 256
 SUB = 8
 AUX = 16
+CHUNKS = 8
 NY = 2
 MIB = 1 << 20
 ROW_SUB, ROW_LANE, ROW_KEEP, ROW_LAST, COL_SUB, COL_LANE, COL_KEEP, COL_LAST = range(8)
@@ -27,9 +28,31 @@
 
 
 def cluster_row(ref, cluster):
+    return ref[pl.ds(cluster, 1), :]
+
+
+def halves_row(ref, cluster):
     first = ref[pl.ds(2 * cluster, 1), :]
     second = ref[pl.ds(2 * cluster + 1, 1), :]
     return jnp.concatenate([first, second], axis=1)
+
+
+def put_halves(ref, cluster, row):
+    ref[pl.ds(2 * cluster, 1), :] = row[:, :128]
+    ref[pl.ds(2 * cluster + 1, 1), :] = row[:, 128:]
+
+
+def squared_norm(cells):
+    wide = cells.astype(jnp.float32)
+    return jnp.sum(wide * wide, axis=0, keepdims=True)
+
+
+def far_offset(axis, j, n):
+    if axis == "tgt":
+        return n // 2 + lax.div(j + 1, 2) * (1 - 2 * lax.rem(j, 2))
+    i = lax.div(j, 2)
+    near = n // 4 + lax.div(i + 1, 2) * (2 * lax.rem(i, 2) - 1)
+    return near + lax.rem(j, 2) * (n - 2 * near)
 
 
 def aux_rows(row, offset, other):
@@ -43,13 +66,14 @@
 
 
 def kernel(
-    sizes, table, x_cells, y_cells, u0, v0, x_mass, y_mass, u_out, v_out, out,
-    xs, ys, u1, v1, parts, helds, slot_m, slot_s, slot_n, slot_d, send_a, send_y, den, held_d,
+    sizes, table, x_count, y_count, x_cells, y_cells, x_mass, y_mass, u_out, v_out, x_norm_out, y_norm_out, out,
+    xs, ys, x_norm, u0, v0, u1, v1, u2, v2, parts, helds, slot_m, slot_s, slot_n, slot_d, send_a, send_y, den, held_d,
     first_y, ring_a, ring_b, last_y, *sems,
 ):
     n_src, n_tgt, slots = sizes
     step = math.gcd(slots, 16)
     features = x_cells.shape[0]
+    clusters = x_cells.shape[1] // TILE
     me_src, me_tgt = lax.axis_index("src"), lax.axis_index("tgt")
     barrier = pltpu.get_barrier_semaphore()
     for axis, me, n in (("tgt", me_tgt, n_tgt), ("src", me_src, n_src)):
@@ -73,12 +97,13 @@
             score = lax.dot_general(left, right, (((0,), (0,)), ((), ())), preferred_element_type=jnp.float32)
             hold = keep.astype(jnp.float32)
             if kind == "max":
-                score = score.reshape(TILE // SUB, SUB, TILE)
-                best = jnp.max(score, axis=0)
-                part = jnp.sum(jnp.exp(score - best[None]), axis=0)
+                score = score.reshape(CHUNKS, TILE // SUB // CHUNKS, SUB, TILE)
+                best = [jnp.max(score[q], axis=0) for q in range(CHUNKS)]
                 old = carry[0] * hold + (1.0 - hold) * EMPTY
-                new = jnp.maximum(old, best)
-                total = carry[1] * hold * jnp.exp(old - new) + part * jnp.exp(best - new)
+                new = functools.reduce(jnp.maximum, best, old)
+                total = carry[1] * hold * jnp.exp(old - new)
+                for q in range(CHUNKS):
+                    total = total + jnp.sum(jnp.exp(score[q] - best[q][None]), axis=0) * jnp.exp(best[q] - new)
                 slot_m[p] = new
                 slot_s[p] = total
                 return new, total
@@ -113,84 +138,126 @@
             start = (jnp.zeros((features, TILE), jnp.float32), jnp.zeros((1, TILE), jnp.float32))
         lax.fori_loop(0, slots // step, group, start)
 
-    def reduce(kind, which, axis, me, n, last, old, mass, new):
+    def reduce(kind, which, axis, me, n, last, old, mass, count, new, meanwhile):
         part, held = parts.at[which], helds.at[which]
-        rows = old.shape[0] // n
-        per = rows // 2
-
-        def finish(c):
-            at = entry(last, c)
-            if kind == "max":
-                best = jnp.max(slot_m[at], axis=0, keepdims=True)
-                row = jnp.sum(slot_s[at] * jnp.exp(slot_m[at] - best), axis=0, keepdims=True)
-                value = best + jnp.log(jnp.where(row > 0.0, row, 1.0))
-            else:
-                value = jnp.sum(slot_s[at], axis=0, keepdims=True)
-            part[pl.ds(2 * c, 1), :] = value[:, :128]
-            part[pl.ds(2 * c + 1, 1), :] = value[:, 128:]
-
-        def finish_group(g):
+        per = clusters // n
+        lanes = lax.broadcasted_iota(jnp.int32, (1, TILE), 1)
+
+        def shard(peer):
+            return pl.ds(pl.multiple_of(peer * per, per), per)
+
+        def finish(peer):
+            rows = []
             for r in range(per):
-                finish(g * per + r)
-
-        pl.loop(0, n)(finish_group)
+                at = entry(last, peer * per + r)
+                if kind == "max":
+                    best = jnp.max(slot_m[at], axis=0, keepdims=True)
+                    row = jnp.sum(slot_s[at] * jnp.exp(slot_m[at] - best), axis=0, keepdims=True)
+                    rows.append(best + jnp.log(jnp.where(row > 0.0, row, 1.0)))
+                else:
+                    rows.append(jnp.sum(slot_s[at], axis=0, keepdims=True))
+            part[shard(peer), :] = jnp.concatenate(rows, axis=0)
+
+        def copy(j, phase):
+            k = far_offset(axis, j, n)
+            peer = lax.rem(me + k, n)
+            mine = shard(me)
+            src_ref, dst_ref = (part.at[shard(peer)], held.at[k]) if phase == 0 else (new.at[mine], new.at[mine])
+            return pltpu.make_async_remote_copy(
+                src_ref=src_ref, dst_ref=dst_ref,
+                send_sem=sems[2 * phase].at[which, k], recv_sem=sems[2 * phase + 1].at[which, k],
+                device_id={axis: peer}, device_id_type=MESH)
+
         if which == 0:
             pl.semaphore_wait(barrier, n_src + n_tgt - 2)
-        mine = pl.ds(pl.multiple_of(me * rows, rows), rows)
-
-        def share(src_ref, dst_ref, phase):
-            made = []
-            for k in range(1, n):
-                peer = lax.rem(me + k, n)
-                copy = pltpu.make_async_remote_copy(
-                    src_ref=src_ref(peer), dst_ref=dst_ref(k),
-                    send_sem=sems[2 * phase].at[which, k], recv_sem=sems[2 * phase + 1].at[which, k],
-                    device_id={axis: peer}, device_id_type=MESH)
-                copy.start()
-                made.append(copy)
-            return made
-
-        made = share(lambda peer: part.at[pl.ds(pl.multiple_of(peer * rows, rows), rows)],
-                     lambda k: held.at[pl.ds(k * rows, rows)], 0)
-        for copy in made:
-            copy.wait_recv()
+
+        @pl.loop(0, n - 1)
+        def _(j):
+            finish(lax.rem(me + far_offset(axis, j, n), n))
+            copy(j, 0).start()
+
+        finish(me)
+        meanwhile()
+        rows = []
+        for r in range(per):
+            c = me * per + r
+            rows.append(jnp.where(lanes < count[c], jnp.log(halves_row(mass, c)), EMPTY))
+        logmass = jnp.concatenate(rows, axis=0)
+
+        @pl.loop(0, n - 1)
+        def _(j):
+            copy(j, 0).wait_recv()
+
+        mine = shard(me)
         own = part[mine, :]
         if kind == "max":
             best = own
             for k in range(1, n):
-                best = jnp.maximum(best, held[k * rows:(k + 1) * rows])
+                best = jnp.maximum(best, held[k])
             total = jnp.exp(own - best)
             for k in range(1, n):
-                total = total + jnp.exp(held[k * rows:(k + 1) * rows] - best)
+                total = total + jnp.exp(held[k] - best)
             lse = best + jnp.log(total)
         else:
             total = own
             for k in range(1, n):
-                total = total + held[k * rows:(k + 1) * rows]
+                total = total + held[k]
             lse = jnp.log(jnp.where(total > 0.0, total, 1.0))
-        logmass = mass[mine, :]
         new[mine, :] = jnp.where(logmass > 0.5 * EMPTY, old[mine, :] + logmass - lse, EMPTY)
-        sent = share(lambda peer: new.at[mine], lambda k: new.at[mine], 1)
-        for copy in made:
-            copy.wait_send()
-        for copy in sent:
-            copy.wait()
-
-    def arrange(c):
-        lanes = pl.ds(pl.multiple_of(c * TILE, TILE), TILE)
-        xs[c] = x_cells[:, lanes] * jnp.bfloat16(4.0)
-        ys[c] = y_cells[:, lanes]
-
-    pl.loop(0, x_cells.shape[1] // TILE)(arrange)
+
+        @pl.loop(0, n - 1)
+        def _(j):
+            copy(j, 1).start()
+
+        @pl.loop(0, n - 1)
+        def _(j):
+            copy(j, 0).wait_send()
+
+        @pl.loop(0, n - 1)
+        def _(j):
+            copy(j, 1).wait()
+
+    lane = lax.broadcasted_iota(jnp.int32, (1, TILE), 1)
+    u0[...] = jnp.zeros(u0.shape, jnp.float32)
+
+    @pl.loop(0, clusters // SUB)
+    def _(g):
+        rows = []
+        for r in range(SUB):
+            c = g * SUB + r
+            at = pl.ds(pl.multiple_of(c * TILE, TILE), TILE)
+            xs[c] = x_cells[:, at] * jnp.bfloat16(4.0)
+            cells = y_cells[:, at]
+            ys[c] = cells
+            rows.append(jnp.where(lane < y_count[c], -2.0 * squared_norm(cells), EMPTY))
+        v0[pl.ds(pl.multiple_of(g * SUB, SUB), SUB), :] = jnp.concatenate(rows, axis=0)
+
+    def norms():
+        @pl.loop(0, clusters // SUB)
+        def _(g):
+            for r in range(SUB):
+                c = g * SUB + r
+                put_halves(x_norm_out, c, squared_norm(xs[c]) * 0.0625)
+                put_halves(y_norm_out, c, -0.5 * cluster_row(v0, c))
+
+    def nothing():
+        pass
+
+    def write_u():
+        @pl.loop(0, clusters // SUB)
+        def _(g):
+            for r in range(SUB):
+                put_halves(u_out, g * SUB + r, cluster_row(u2, g * SUB + r))
+
     sweep("max", ROW_SUB, ys, xs, v0, u0)
-    reduce("max", 0, "tgt", me_tgt, n_tgt, ROW_LAST, u0, x_mass, u1)
+    reduce("max", 0, "tgt", me_tgt, n_tgt, ROW_LAST, u0, x_mass, x_count, u1, nothing)
     sweep("max", COL_SUB, xs, ys, u1, v0)
-    reduce("max", 1, "src", me_src, n_src, COL_LAST, v0, y_mass, v1)
+    reduce("max", 1, "src", me_src, n_src, COL_LAST, v0, y_mass, y_count, v1, norms)
     sweep("sum", ROW_SUB, ys, xs, v1, u1)
-    reduce("sum", 2, "tgt", me_tgt, n_tgt, ROW_LAST, u1, x_mass, u_out)
-    sweep("sum", COL_SUB, xs, ys, u_out, v1)
-    reduce("sum", 3, "src", me_src, n_src, COL_LAST, v1, y_mass, v_out)
-    sweep("map", ROW_SUB, ys, xs, v_out, u_out)
+    reduce("sum", 2, "tgt", me_tgt, n_tgt, ROW_LAST, u1, x_mass, x_count, u2, nothing)
+    sweep("sum", COL_SUB, xs, ys, u2, v1)
+    reduce("sum", 3, "src", me_src, n_src, COL_LAST, v1, y_mass, y_count, v2, write_u)
+    sweep("map", ROW_SUB, ys, xs, v2, u2)
 
     n, nz = n_tgt, n_tgt // NY
     z, y = me_tgt // NY, lax.rem(me_tgt, NY)
@@ -217,13 +284,14 @@
 
     partner = z * NY + other
     over_y = [[None] * nz for _ in sign]
-    over_a = [[None] * nz for _ in sign]
+    over_a = [[[None] * nz for _ in range(NY)] for _ in sign]
     over_b = [[None] * nz for _ in sign]
-    for d in range(2):
-        for side in range(NY):
+    sides = (other, y)
+    for s in range(NY):
+        for d in range(2):
             for c in range(half):
-                send_a[d, side, c] = own(block(d, 0), side, d * half, c)
-        over_a[d][0] = copy(send_a.at[d], ring_a.at[d, 0], 3, d * nz, device(z + sign[d]))
+                send_a[d, s, c] = own(block(d, 0), sides[s], d * half, c)
+            over_a[d][s][0] = copy(send_a.at[d, s], ring_a.at[d, 0, s], 3, (d * NY + s) * nz, device(z + sign[d]))
     for hop in range(nz):
         for d in range(2):
             for c in range(half):
@@ -239,6 +307,7 @@
     for k in range(1, n):
         peer = lax.rem(me_tgt + k, n)
         others.append(copy(den.at[peer], held_d.at[k], 6, k, peer))
+    over_last = []
     for hop in range(nz):
         at = [block(d, hop) for d in range(2)]
         for d in range(2):
@@ -252,14 +321,24 @@
                 first_y[d, hop, c] = value
             if hop < nz - 1:
                 over_b[d][hop] = copy(first_y.at[d, hop], ring_b.at[d, hop], 4, d * nz + hop, device(z + sign[d]))
-            if hop > 0:
-                over_a[d][hop - 1].wait_recv()
-                for side in range(NY):
-                    for c in range(half):
-                        ring_a[d, hop - 1, side, c] += own(at[d], side, d * half, c)
-            if 0 < hop < nz - 1:
-                over_a[d][hop] = copy(ring_a.at[d, hop - 1], ring_a.at[d, hop], 3, d * nz + hop, device(z + sign[d]))
-    over_last = [copy(ring_a.at[d, nz - 2, other], last_y.at[d], 5, d, partner) for d in range(2)]
+        for s in range(NY):
+            for d in range(2):
+                if hop == 0:
+                    continue
+                over_a[d][s][hop - 1].wait_recv()
+                for c in range(half):
+                    ring_a[d, hop - 1, s, c] += own(at[d], sides[s], d * half, c)
+                if hop < nz - 1:
+                    over_a[d][s][hop] = copy(
+                        ring_a.at[d, hop - 1, s], ring_a.at[d, hop, s], 3, (d * NY + s) * nz + hop, device(z + sign[d]))
+                elif s == 0:
+                    over_last.append(copy(ring_a.at[d, nz - 2, 0], last_y.at[d], 5, d, partner))
+
+    @pl.loop(0, clusters // SUB)
+    def _(g):
+        for r in range(SUB):
+            put_halves(v_out, g * SUB + r, cluster_row(v2, g * SUB + r))
+
     for made in others:
         made.wait_recv()
     total = den[me_tgt]
@@ -276,36 +355,37 @@
     for d in range(2):
         over_last[d].wait_recv()
         for c in range(half):
-            put(d * half + c, ring_a[d, nz - 2, y, c] + last_y[d, c])
+            put(d * half + c, ring_a[d, nz - 2, 1, c] + last_y[d, c])
     for made in others + over_last:
         made.wait_send()
     for d in range(2):
         for hop in range(nz):
             over_y[d][hop].wait_send()
         for hop in range(nz - 1):
-            over_a[d][hop].wait_send()
+            for s in range(NY):
+                over_a[d][s][hop].wait_send()
             over_b[d][hop].wait_send()
 
 
-def transport(n_src, n_tgt, slots, table, x_cells, y_cells, u0, v0, x_mass, y_mass):
+def transport(n_src, n_tgt, slots, table, x_count, y_count, x_cells, y_cells, x_mass, y_mass):
     features = x_cells.shape[0]
     clusters = x_cells.shape[1] // TILE
     per, nz = clusters // n_tgt, n_tgt // NY
     quarter = per // 4
     f32 = jnp.float32
     vmem = pl.BlockSpec(memory_space=pltpu.VMEM)
+    smem = pl.BlockSpec(memory_space=pltpu.SMEM)
     dma = pltpu.SemaphoreType.DMA
     most = max(n_src, n_tgt)
     sems = [dma((4, most))] * 4
-    for many in (2 * nz, 2 * nz, 2 * nz, 2, n_tgt):
+    for many in (2 * nz, 2 * NY * nz, 2 * nz, 2, n_tgt):
         sems += [dma((many,))] * 2
-    scratch = [
-        pltpu.VMEM((clusters, features, TILE), jnp.bfloat16),
-        pltpu.VMEM((clusters, features, TILE), jnp.bfloat16),
-        pltpu.VMEM(u0.shape, f32),
-        pltpu.VMEM(v0.shape, f32),
-        pltpu.VMEM((4,) + u0.shape, f32),
-        pltpu.VMEM((4,) + u0.shape, f32),
+    flat = jax.ShapeDtypeStruct((2 * clusters, TILE // 2), f32)
+    row = pltpu.VMEM((clusters, TILE), f32)
+    cells = pltpu.VMEM((clusters, features, TILE), jnp.bfloat16)
+    scratch = [cells, cells] + [row] * 7 + [
+        pltpu.VMEM((4, clusters, TILE), f32),
+        pltpu.VMEM((4, most, clusters // min(n_src, n_tgt), TILE), f32),
         pltpu.VMEM((slots + 1, SUB, TILE), f32),
         pltpu.VMEM((slots + 1, SUB, TILE), f32),
         pltpu.VMEM((slots + 1, features, TILE), f32),
@@ -321,17 +401,13 @@
     ]
     return pl.pallas_call(
         functools.partial(kernel, (n_src, n_tgt, slots)),
-        out_shape=(
-            jax.ShapeDtypeStruct(u0.shape, f32),
-            jax.ShapeDtypeStruct(v0.shape, f32),
-            jax.ShapeDtypeStruct((features, per * TILE), f32),
-        ),
-        in_specs=[pl.BlockSpec(memory_space=pltpu.SMEM)] + [vmem] * 6,
-        out_specs=(vmem, vmem, vmem),
+        out_shape=(flat,) * 4 + (jax.ShapeDtypeStruct((features, per * TILE), f32),),
+        in_specs=[smem] * 3 + [vmem] * 4,
+        out_specs=(vmem,) * 5,
         scratch_shapes=scratch + sems,
         compiler_params=pltpu.CompilerParams(collective_id=0, has_side_effects=True, vmem_limit_bytes=40 * MIB),
         name="transport",
-    )(table, x_cells, y_cells, u0, v0, x_mass, y_mass)
+    )(table, x_count, y_count, x_cells, y_cells, x_mass, y_mass)
 
 
 def pair_tables(pair_lists, tgt_block, per_block, slots):
@@ -364,28 +440,15 @@
     return jnp.concatenate([row_tgt, row_src, row_keep, row_last, col_src, col_tgt, col_keep, col_last])
 
 
-def side(cells, mass, count):
-    clusters = count.shape[0]
-    wide = cells.astype(jnp.float32)
-    norm = jnp.sum(wide * wide, axis=0).reshape(2 * clusters, 128)
-    place = jnp.arange(2, dtype=jnp.int32)[None, :, None] * 128 + jnp.arange(128, dtype=jnp.int32)[None, None, :]
-    live = (place < count[:, None, None]).reshape(2 * clusters, 128)
-    logmass = jnp.where(live, jnp.log(mass).reshape(2 * clusters, 128), EMPTY)
-    return norm, live, logmass
-
-
 def shards(source_cells, target_cells, source_mass, target_mass, source_count, target_count, pair_lists):
     n_src, n_tgt = lax.axis_size("src"), lax.axis_size("tgt")
     slots = 2 * pair_lists.size // n_tgt
     table = pair_tables(pair_lists, lax.axis_index("tgt"), target_count.shape[0], slots)
-    src_norm, src_live, src_logmass = side(source_cells, source_mass, source_count)
-    tgt_norm, tgt_live, tgt_logmass = side(target_cells, target_mass, target_count)
-    u0 = -2.0 * src_norm
-    v0 = jnp.where(tgt_live, -2.0 * tgt_norm, EMPTY)
-    u, v, mapped = transport(
-        n_src, n_tgt, slots, table, source_cells, target_cells, u0, v0, src_logmass, tgt_logmass)
-    source_pot = jnp.where(src_live, 0.5 * u + src_norm, 0.0)
-    target_pot = jnp.where(tgt_live, 0.5 * v + tgt_norm, 0.0)
+    u, v, x_norm, y_norm, mapped = transport(
+        n_src, n_tgt, slots, table, source_count, target_count, source_cells, target_cells,
+        source_mass.reshape(-1, TILE // 2), target_mass.reshape(-1, TILE // 2))
+    source_pot = jnp.where(u > 0.5 * EMPTY, 0.5 * u + x_norm, 0.0)
+    target_pot = jnp.where(v > 0.5 * EMPTY, 0.5 * v + y_norm, 0.0)
     return source_pot.reshape(-1), target_pot.reshape(-1), mapped
 
 

time: 165 us -> 155 us (0.939)
  Pallas kernels: 151 us -> 139 us
  local copies, waits for them, and re-layouts: 4.5 us -> 8.24 us
  other arithmetic: 7.88 us -> 5.22 us
    pallas_call x1, Pallas kernels: 151 us -> 139 us  [transport(): pl.pallas_call(functools.partial(kernel, (n_src, n_tgt, slots)), out_shap...]
    unnamed x10 -> x14, local copies, waits for them, and re-layouts: 2.26 us -> 7.79 us
    reduce_sum x2 -> x0, other arithmetic: 2.87 us -> none  [side(): norm = jnp.sum(wide * wide, axis=0).reshape(2 * clusters, 128)]
    lt x5 -> x0, local copies, waits for them, and re-layouts: 1.79 us -> none  [side(): live = (place < count[:, None, None]).reshape(2 * clusters, 128)]
where the time goes in v5:
time: 155 us; the launch traced here: 154 us
  Pallas kernels  139 us (90%)
  local copies, waits for them, and re-layouts  8.24 us (5%)
  other arithmetic  5.22 us (3%)
    pallas_call x1, Pallas kernels, transport(): pl.pallas_call(functools.partial(kernel, (n_src, n_tgt, slots)), out_shap...  139 us
    unnamed x14, local copies, waits for them, and re-layouts  7.79 us

profile of v5, /device:TPU:24, one launch (start us, length us, event | category | flops | bytes accessed | tf_op | source)
XLA Modules:
  0.0 153.6 jit_solution(4889458303860577720)
XLA Ops:
  0.6 1.3 convert_reduce_fusion.1
  2.0 0.6 iota_compare_fusion.5
  2.6 0.8 copy.13
  3.4 0.1 reshape.136
  3.5 0.1 reshape.134
  3.6 0.3 reduce-window.9
  3.9 0.1 slice.19
  4.0 0.1 slice_reduce_fusion
  4.1 0.1 add_bitcast_fusion
  4.2 0.2 select_reduce_fusion
  4.4 0.1 compare_convert_fusion.1
  4.5 0.2 convert_reduce_fusion
  4.7 0.7 iota_select_fusion
  5.4 0.1 select_reduce_fusion.3
  5.5 0.1 compare_convert_fusion
  5.5 0.2 select_reduce_fusion.2
  5.7 0.1 concatenate.3.table
  5.8 0.0 copy-start
  5.8 1.6 %copy-done = bf16[32,32768]{1,0:T(8,128)(2,1)S(1)} copy-done((bf16[32,32768]{1,0:T(8,128)(2,1)S(1)}, bf16[32,32768]{1,0:T(8,128)(2,1)}, u32[]{:S(2)}) %copy-start) | copy-done | bytes 2097176
  7.4 0.0 copy-start.1
  7.4 1.6 %copy-done.1 = bf16[32,32768]{1,0:T(8,128)(2,1)S(1)} copy-done((bf16[32,32768]{1,0:T(8,128)(2,1)S(1)}, bf16[32,32768]{1,0:T(8,128)(2,1)}, u32[]{:S(2)}) %copy-start.1) | copy-done | bytes 2097176
  9.0 0.0 copy-start.2
  9.0 0.9 copy-done.2
  9.9 0.0 copy-start.3
  9.9 0.9 copy-done.3
  10.8 0.0 copy-start.4
  10.8 0.7 copy-done.4
  11.4 0.0 copy-start.5
  11.4 0.7 copy-done.5
  12.1 139.4 %transport.1 = (f32[256,128]{1,0:T(8,128)S(1)}, f32[256,128]{1,0:T(8,128)S(1)}, f32[256,128]{1,0:T(8,128)S(1)}, f32[256,128]{1,0:T(8,128)S(1)}, f32[32,2048]{1,0:T(8,128)S(1)}) custom-call(s32[1024]{0:T(1024)S(1)} %concatenate.3.table, s32[128]{0:T(128)S(1)} %copy-done.4, s32[128]{0:T(128)S(1)} %copy-done.5, bf16[32,32768]{1,0:T(8,128)(2,1)S(1)} %copy-done, ...), custom_call_target="tpu_custom_call" | custom-call | tf_op jit(solution)/shard_map/transport/pallas_call | solution.py:402
  151.5 0.7 select_bitcast_fusion.1
  152.2 0.7 select_bitcast_fusion
  152.9 0.7 copy.16
  (6 shorter events, 0.1 us)
Async XLA Ops:
  5.8 1.6 %copy-start = (bf16[32,32768]{1,0:T(8,128)(2,1)S(1)}, bf16[32,32768]{1,0:T(8,128)(2,1)}, u32[]{:S(2)}) copy-start(bf16[32,32768]{1,0:T(8,128)(2,1)} %x_cells.1) | copy-start | bytes 6291460
  7.4 1.6 %copy-start.1 = (bf16[32,32768]{1,0:T(8,128)(2,1)S(1)}, bf16[32,32768]{1,0:T(8,128)(2,1)}, u32[]{:S(2)}) copy-start(bf16[32,32768]{1,0:T(8,128)(2,1)} %y_cells.1) | copy-start | bytes 6291460
  9.0 0.9 copy-start.2
  9.9 0.9 copy-start.3
  10.8 0.7 copy-start.4
  11.4 0.7 copy-start.5

commit v6 on v5

--- a/solution.py
+++ b/solution.py
@@ -14,9 +14,10 @@
 SUB = 8
 AUX = 16
 CHUNKS = 8
+CODE = 32752.0
 NY = 2
 MIB = 1 << 20
-ROW_SUB, ROW_LANE, ROW_KEEP, ROW_LAST, COL_SUB, COL_LANE, COL_KEEP, COL_LAST = range(8)
+ROW_SUB, ROW_LANE, ROW_KEEP, ROW_LAST, COL_SUB, COL_LANE, COL_KEEP, COL_LAST, SRC_COUNT, TGT_COUNT = range(10)
 
 
 def split3(row):
@@ -66,20 +67,26 @@
 
 
 def kernel(
-    sizes, table, x_count, y_count, x_cells, y_cells, x_mass, y_mass, u_out, v_out, x_norm_out, y_norm_out, out,
-    xs, ys, x_norm, u0, v0, u1, v1, u2, v2, parts, helds, slot_m, slot_s, slot_n, slot_d, send_a, send_y, den, held_d,
-    first_y, ring_a, ring_b, last_y, *sems,
+    sizes, table, xs, ys, x_mass, y_mass, u_out, v_out, x_norm_out, y_norm_out, out,
+    masses, u0, v0, u1, v1, u2, v2, parts, helds, slot_m, slot_s, slot_n, slot_d, send_a, send_y, den, held_d,
+    first_y, ring_a, ring_b, last_y, kept, local, *sems,
 ):
     n_src, n_tgt, slots = sizes
     step = math.gcd(slots, 16)
-    features = x_cells.shape[0]
-    clusters = x_cells.shape[1] // TILE
+    clusters, features = xs.shape[:2]
     me_src, me_tgt = lax.axis_index("src"), lax.axis_index("tgt")
     barrier = pltpu.get_barrier_semaphore()
     for axis, me, n in (("tgt", me_tgt, n_tgt), ("src", me_src, n_src)):
         for k in range(1, n):
             pl.semaphore_signal(barrier, inc=1, device_id={axis: lax.rem(me + k, n)}, device_id_type=MESH)
 
+    fetches = []
+    for i, (mass, me, n) in enumerate(((x_mass, me_tgt, n_tgt), (y_mass, me_src, n_src))):
+        rows = 2 * clusters // n
+        fetch = pltpu.make_async_copy(
+            mass.at[pl.ds(pl.multiple_of(me * rows, rows), rows)], masses.at[i], local.at[i])
+        fetch.start()
+        fetches.append(fetch)
     slot_m[slots] = jnp.full((SUB, TILE), EMPTY, jnp.float32)
     slot_s[slots] = jnp.zeros((SUB, TILE), jnp.float32)
     slot_n[slots] = jnp.zeros((features, TILE), jnp.float32)
@@ -88,12 +95,15 @@
     def entry(which, p):
         return table[which * slots + p]
 
+    def scaled(cells, ref):
+        return cells * jnp.bfloat16(4.0) if ref is xs else cells
+
     def sweep(kind, first, sub_cells, lane_cells, sub_pot, lane_pot):
         def tile(p, carry):
             a, b, keep = entry(first, p), entry(first + 1, p), entry(first + 2, p)
             sub, lane = sub_cells[a], lane_cells[b]
-            left = jnp.concatenate([sub, aux_rows(cluster_row(sub_pot, a), 0, 3)], axis=0)
-            right = jnp.concatenate([lane, aux_rows(cluster_row(lane_pot, b), 3, 0)], axis=0)
+            left = jnp.concatenate([scaled(sub, sub_cells), aux_rows(cluster_row(sub_pot, a), 0, 3)], axis=0)
+            right = jnp.concatenate([scaled(lane, lane_cells), aux_rows(cluster_row(lane_pot, b), 3, 0)], axis=0)
             score = lax.dot_general(left, right, (((0,), (0,)), ((), ())), preferred_element_type=jnp.float32)
             hold = keep.astype(jnp.float32)
             if kind == "max":
@@ -138,7 +148,7 @@
             start = (jnp.zeros((features, TILE), jnp.float32), jnp.zeros((1, TILE), jnp.float32))
         lax.fori_loop(0, slots // step, group, start)
 
-    def reduce(kind, which, axis, me, n, last, old, mass, count, new, meanwhile):
+    def reduce(kind, which, axis, me, n, last, old, new, meanwhile):
         part, held = parts.at[which], helds.at[which]
         per = clusters // n
         lanes = lax.broadcasted_iota(jnp.int32, (1, TILE), 1)
@@ -178,10 +188,13 @@
 
         finish(me)
         meanwhile()
+        if which < 2:
+            fetches[which].wait()
+        mass = masses.at[which % 2]
+        count = (SRC_COUNT, TGT_COUNT)[which % 2]
         rows = []
         for r in range(per):
-            c = me * per + r
-            rows.append(jnp.where(lanes < count[c], jnp.log(halves_row(mass, c)), EMPTY))
+            rows.append(jnp.where(lanes < entry(count, me * per + r), jnp.log(halves_row(mass, r)), EMPTY))
         logmass = jnp.concatenate(rows, axis=0)
 
         @pl.loop(0, n - 1)
@@ -225,11 +238,7 @@
         rows = []
         for r in range(SUB):
             c = g * SUB + r
-            at = pl.ds(pl.multiple_of(c * TILE, TILE), TILE)
-            xs[c] = x_cells[:, at] * jnp.bfloat16(4.0)
-            cells = y_cells[:, at]
-            ys[c] = cells
-            rows.append(jnp.where(lane < y_count[c], -2.0 * squared_norm(cells), EMPTY))
+            rows.append(jnp.where(lane < entry(TGT_COUNT, c), -2.0 * squared_norm(ys[c]), EMPTY))
         v0[pl.ds(pl.multiple_of(g * SUB, SUB), SUB), :] = jnp.concatenate(rows, axis=0)
 
     def norms():
@@ -237,7 +246,7 @@
         def _(g):
             for r in range(SUB):
                 c = g * SUB + r
-                put_halves(x_norm_out, c, squared_norm(xs[c]) * 0.0625)
+                put_halves(x_norm_out, c, squared_norm(xs[c]))
                 put_halves(y_norm_out, c, -0.5 * cluster_row(v0, c))
 
     def nothing():
@@ -250,30 +259,34 @@
                 put_halves(u_out, g * SUB + r, cluster_row(u2, g * SUB + r))
 
     sweep("max", ROW_SUB, ys, xs, v0, u0)
-    reduce("max", 0, "tgt", me_tgt, n_tgt, ROW_LAST, u0, x_mass, x_count, u1, nothing)
+    reduce("max", 0, "tgt", me_tgt, n_tgt, ROW_LAST, u0, u1, nothing)
     sweep("max", COL_SUB, xs, ys, u1, v0)
-    reduce("max", 1, "src", me_src, n_src, COL_LAST, v0, y_mass, y_count, v1, norms)
+    reduce("max", 1, "src", me_src, n_src, COL_LAST, v0, v1, norms)
     sweep("sum", ROW_SUB, ys, xs, v1, u1)
-    reduce("sum", 2, "tgt", me_tgt, n_tgt, ROW_LAST, u1, x_mass, x_count, u2, nothing)
+    reduce("sum", 2, "tgt", me_tgt, n_tgt, ROW_LAST, u1, u2, nothing)
     sweep("sum", COL_SUB, xs, ys, u2, v1)
-    reduce("sum", 3, "src", me_src, n_src, COL_LAST, v1, y_mass, y_count, v2, write_u)
+    reduce("sum", 3, "src", me_src, n_src, COL_LAST, v1, v2, write_u)
     sweep("map", ROW_SUB, ys, xs, v2, u2)
 
     n, nz = n_tgt, n_tgt // NY
     z, y = me_tgt // NY, lax.rem(me_tgt, NY)
     other = NY - 1 - y
+    sides = (other, y)
     per = out.shape[1] // TILE
-    half = per // 4
+    half = per // 2
     sign = (1, -1)
-
-    def device(at):
-        return lax.rem(at + nz, nz) * NY + y
-
-    def block(d, hop):
-        return lax.rem(z - sign[d] * (1 + hop) + 2 * nz, nz)
-
-    def own(at, side, base, c):
-        return slot_n[entry(ROW_LAST, (at * NY + side) * per + base + c)]
+    far = nz // 2
+    hops = ((far, nz - 1 - far), (nz - 1 - far, far))
+    partner = z * NY + other
+
+    def toward(d):
+        return lax.rem(z + sign[d] + nz, nz) * NY + y
+
+    def block(g, d, hop):
+        return lax.rem(z + sign[d] * (hops[g][d] - hop) + nz, nz)
+
+    def own(at, side, g, c):
+        return slot_n[entry(ROW_LAST, (at * NY + side) * per + g * half + c)]
 
     def copy(src, dst, sem, k, peer):
         made = pltpu.make_async_remote_copy(
@@ -282,21 +295,44 @@
         made.start()
         return made
 
-    partner = z * NY + other
-    over_y = [[None] * nz for _ in sign]
-    over_a = [[[None] * nz for _ in range(NY)] for _ in sign]
-    over_b = [[None] * nz for _ in sign]
-    sides = (other, y)
-    for s in range(NY):
-        for d in range(2):
-            for c in range(half):
-                send_a[d, s, c] = own(block(d, 0), sides[s], d * half, c)
-            over_a[d][s][0] = copy(send_a.at[d, s], ring_a.at[d, 0, s], 3, (d * NY + s) * nz, device(z + sign[d]))
-    for hop in range(nz):
-        for d in range(2):
-            for c in range(half):
-                send_y[d, hop, c] = own(block(d, hop), other, (2 + d) * half, c)
-            over_y[d][hop] = copy(send_y.at[d, hop], first_y.at[d, hop], 2, d * nz + hop, partner)
+    def encode(ref, values):
+        exponents = []
+        for c in range(half):
+            value = values(c)
+            largest = jnp.max(jnp.abs(value), axis=0, keepdims=True)
+            exponent = jnp.ceil(jnp.log2(jnp.maximum(largest, 1e-30)))
+            code = jnp.floor(value * (jnp.exp2(-exponent) * CODE) + 0.5)
+            ref[c * features:(c + 1) * features, :] = code.astype(jnp.int32).astype(jnp.int16)
+            exponents.append(exponent)
+        exponents.append(jnp.zeros((AUX - half, TILE), jnp.float32))
+        block = jnp.concatenate(exponents, axis=0)
+        ref[half * features:half * features + AUX, :] = block.astype(jnp.int32).astype(jnp.int16)
+
+    def decoder(ref):
+        exponents = ref[half * features:half * features + AUX, :].astype(jnp.int32).astype(jnp.float32)
+        scale = jnp.exp2(exponents) * (1.0 / CODE)
+        return lambda c: (
+            ref[c * features:(c + 1) * features, :].astype(jnp.int32).astype(jnp.float32) * scale[c:c + 1])
+
+    pieces = [(d, hop) for hop in range(far) for d in range(2) if hop < hops[1][d]]
+    over_y = {}
+    over_a = {}
+    over_b = {}
+
+    def send_piece(i, at):
+        encode(send_y.at[i], lambda c: own(at, other, 1, c))
+        over_y[i] = copy(send_y.at[i], first_y.at[i], 2, i, partner)
+
+    for i in range(2):
+        d, hop = pieces[i]
+        send_piece(i, block(1, d, hop))
+        for s in range(NY):
+            encode(send_a.at[i, s], lambda c: own(block(0, i, 0), sides[s], 0, c))
+            over_a[i, s, 0] = copy(send_a.at[i, s], ring_a.at[i, 0, s], 3, (i * NY + s) * far, toward(i))
+    for i in range(2, nz - 1):
+        d, hop = pieces[i]
+        send_piece(i, block(1, d, hop))
+    send_piece(nz - 1, z)
 
     def gather(t):
         for c in range(per):
@@ -307,32 +343,44 @@
     for k in range(1, n):
         peer = lax.rem(me_tgt + k, n)
         others.append(copy(den.at[peer], held_d.at[k], 6, k, peer))
-    over_last = []
-    for hop in range(nz):
-        at = [block(d, hop) for d in range(2)]
+
+    def step_b(d, hop):
+        i = pieces.index((d, hop))
+        over_y[i].wait_recv()
+        parts_of = [decoder(first_y.at[i])]
+        if hop > 0:
+            over_b[d, hop - 1].wait_recv()
+            parts_of.append(decoder(ring_b.at[d, hop - 1]))
+        at = block(1, d, hop)
+        encode(first_y.at[i], lambda c: sum((part(c) for part in parts_of), own(at, y, 1, c)))
+        over_b[d, hop] = copy(first_y.at[i], ring_b.at[d, hop], 4, d * far + hop, toward(d))
+
+    def step_a(d, s, hop):
+        over_a[d, s, hop - 1].wait_recv()
+        held = ring_a.at[d, hop - 1, s]
+        arrived = decoder(held)
+        at = block(0, d, hop)
+        encode(held, lambda c: arrived(c) + own(at, sides[s], 0, c))
+        over_a[d, s, hop] = copy(held, ring_a.at[d, hop, s], 3, (d * NY + s) * far + hop, toward(d))
+
+    for hop in range(far):
         for d in range(2):
-            over_y[d][hop].wait_recv()
-            if hop > 0:
-                over_b[d][hop - 1].wait_recv()
-            for c in range(half):
-                value = first_y[d, hop, c] + own(at[d], y, (2 + d) * half, c)
-                if hop > 0:
-                    value = value + ring_b[d, hop - 1, c]
-                first_y[d, hop, c] = value
-            if hop < nz - 1:
-                over_b[d][hop] = copy(first_y.at[d, hop], ring_b.at[d, hop], 4, d * nz + hop, device(z + sign[d]))
+            if hop < hops[1][d]:
+                step_b(d, hop)
         for s in range(NY):
             for d in range(2):
-                if hop == 0:
-                    continue
-                over_a[d][s][hop - 1].wait_recv()
-                for c in range(half):
-                    ring_a[d, hop - 1, s, c] += own(at[d], sides[s], d * half, c)
-                if hop < nz - 1:
-                    over_a[d][s][hop] = copy(
-                        ring_a.at[d, hop - 1, s], ring_a.at[d, hop, s], 3, (d * NY + s) * nz + hop, device(z + sign[d]))
-                elif s == 0:
-                    over_last.append(copy(ring_a.at[d, nz - 2, 0], last_y.at[d], 5, d, partner))
+                if 0 < hop < hops[0][d]:
+                    step_a(d, s, hop)
+
+    def arrived_a(s):
+        both = []
+        for d in range(2):
+            over_a[d, s, hops[0][d] - 1].wait_recv()
+            both.append(decoder(ring_a.at[d, hops[0][d] - 1, s]))
+        return lambda c: both[0](c) + both[1](c) + own(z, sides[s], 0, c)
+
+    encode(kept, arrived_a(0))
+    over_last = copy(kept, last_y, 5, 0, partner)
 
     @pl.loop(0, clusters // SUB)
     def _(g):
@@ -349,68 +397,72 @@
     def put(c, value):
         out[:, c * TILE:(c + 1) * TILE] = value / total[c:c + 1]
 
+    over_y[nz - 1].wait_recv()
+    parts_b = [decoder(first_y.at[nz - 1])]
     for d in range(2):
-        for c in range(half):
-            put((2 + d) * half + c, first_y[d, nz - 1, c])
-    for d in range(2):
-        over_last[d].wait_recv()
-        for c in range(half):
-            put(d * half + c, ring_a[d, nz - 2, 1, c] + last_y[d, c])
-    for made in others + over_last:
+        over_b[d, hops[1][d] - 1].wait_recv()
+        parts_b.append(decoder(ring_b.at[d, hops[1][d] - 1]))
+    for c in range(half):
+        put(half + c, sum((part(c) for part in parts_b), own(z, y, 1, c)))
+    mine = arrived_a(1)
+    over_last.wait_recv()
+    last = decoder(last_y)
+    for c in range(half):
+        put(c, mine(c) + last(c))
+    for made in others + [over_last] + list(over_y.values()) + list(over_a.values()) + list(over_b.values()):
         made.wait_send()
-    for d in range(2):
-        for hop in range(nz):
-            over_y[d][hop].wait_send()
-        for hop in range(nz - 1):
-            for s in range(NY):
-                over_a[d][s][hop].wait_send()
-            over_b[d][hop].wait_send()
-
-
-def transport(n_src, n_tgt, slots, table, x_count, y_count, x_cells, y_cells, x_mass, y_mass):
-    features = x_cells.shape[0]
-    clusters = x_cells.shape[1] // TILE
+
+
+def transport(n_src, n_tgt, slots, table, xs, ys, x_mass, y_mass):
+    clusters, features = xs.shape[:2]
     per, nz = clusters // n_tgt, n_tgt // NY
-    quarter = per // 4
+    far = nz // 2
     f32 = jnp.float32
     vmem = pl.BlockSpec(memory_space=pltpu.VMEM)
     smem = pl.BlockSpec(memory_space=pltpu.SMEM)
+    hbm = pl.BlockSpec(memory_space=pl.ANY)
     dma = pltpu.SemaphoreType.DMA
     most = max(n_src, n_tgt)
     sems = [dma((4, most))] * 4
-    for many in (2 * nz, 2 * NY * nz, 2 * nz, 2, n_tgt):
+    for many in (nz, 2 * NY * far, 2 * far, 1, n_tgt):
         sems += [dma((many,))] * 2
     flat = jax.ShapeDtypeStruct((2 * clusters, TILE // 2), f32)
     row = pltpu.VMEM((clusters, TILE), f32)
-    cells = pltpu.VMEM((clusters, features, TILE), jnp.bfloat16)
-    scratch = [cells, cells] + [row] * 7 + [
+    coded = (per // 2 * features + AUX, TILE)
+
+    def codes(*many):
+        return pltpu.VMEM(many + coded, jnp.int16)
+
+    scratch = [pltpu.VMEM((2, 2 * clusters // n_tgt, TILE // 2), f32)] + [row] * 6 + [
         pltpu.VMEM((4, clusters, TILE), f32),
         pltpu.VMEM((4, most, clusters // min(n_src, n_tgt), TILE), f32),
         pltpu.VMEM((slots + 1, SUB, TILE), f32),
         pltpu.VMEM((slots + 1, SUB, TILE), f32),
         pltpu.VMEM((slots + 1, features, TILE), f32),
         pltpu.VMEM((slots + SUB, TILE), f32),
-        pltpu.VMEM((2, NY, quarter, features, TILE), f32),
-        pltpu.VMEM((2, nz, quarter, features, TILE), f32),
+        codes(2, NY),
+        codes(nz),
         pltpu.VMEM((n_tgt, per, TILE), f32),
         pltpu.VMEM((n_tgt, per, TILE), f32),
-        pltpu.VMEM((2, nz, quarter, features, TILE), f32),
-        pltpu.VMEM((2, nz - 1, NY, quarter, features, TILE), f32),
-        pltpu.VMEM((2, nz - 1, quarter, features, TILE), f32),
-        pltpu.VMEM((2, quarter, features, TILE), f32),
+        codes(nz),
+        codes(2, far, NY),
+        codes(2, far),
+        codes(),
+        codes(),
+        dma((2,)),
     ]
     return pl.pallas_call(
         functools.partial(kernel, (n_src, n_tgt, slots)),
         out_shape=(flat,) * 4 + (jax.ShapeDtypeStruct((features, per * TILE), f32),),
-        in_specs=[smem] * 3 + [vmem] * 4,
+        in_specs=[smem, vmem, vmem, hbm, hbm],
         out_specs=(vmem,) * 5,
         scratch_shapes=scratch + sems,
         compiler_params=pltpu.CompilerParams(collective_id=0, has_side_effects=True, vmem_limit_bytes=40 * MIB),
         name="transport",
-    )(table, x_count, y_count, x_cells, y_cells, x_mass, y_mass)
-
-
-def pair_tables(pair_lists, tgt_block, per_block, slots):
+    )(table, xs, ys, x_mass, y_mass)
+
+
+def pair_tables(pair_lists, tgt_block, per_block, slots, counts):
     width = pair_lists.shape[1]
     flat = pair_lists.reshape(-1)
     chosen = flat // per_block == tgt_block
@@ -437,15 +489,18 @@
 
     row_keep, row_last = ends(row_src)
     col_keep, col_last = ends(col_tgt)
-    return jnp.concatenate([row_tgt, row_src, row_keep, row_last, col_src, col_tgt, col_keep, col_last])
+    return jnp.concatenate([row_tgt, row_src, row_keep, row_last, col_src, col_tgt, col_keep, col_last] + counts)
 
 
 def shards(source_cells, target_cells, source_mass, target_mass, source_count, target_count, pair_lists):
     n_src, n_tgt = lax.axis_size("src"), lax.axis_size("tgt")
     slots = 2 * pair_lists.size // n_tgt
-    table = pair_tables(pair_lists, lax.axis_index("tgt"), target_count.shape[0], slots)
+    table = pair_tables(
+        pair_lists, lax.axis_index("tgt"), target_count.shape[0], slots, [source_count, target_count])
+    xs, ys = (
+        jnp.transpose(cells.reshape(cells.shape[0], -1, TILE), (1, 0, 2)) for cells in (source_cells, target_cells))
     u, v, x_norm, y_norm, mapped = transport(
-        n_src, n_tgt, slots, table, source_count, target_count, source_cells, target_cells,
+        n_src, n_tgt, slots, table, xs, ys,
         source_mass.reshape(-1, TILE // 2), target_mass.reshape(-1, TILE // 2))
     source_pot = jnp.where(u > 0.5 * EMPTY, 0.5 * u + x_norm, 0.0)
     target_pot = jnp.where(v > 0.5 * EMPTY, 0.5 * v + y_norm, 0.0)

time: 155 us -> 139 us (0.90)
  Pallas kernels: 139 us -> 127 us
  local copies, waits for them, and re-layouts: 8.24 us -> 5.47 us
    pallas_call x1, Pallas kernels: 139 us -> 127 us  [transport(): pl.pallas_call(functools.partial(kernel, (n_src, n_tgt, slots)), out_shap...]
    unnamed x14 -> x6, local copies, waits for them, and re-layouts: 7.79 us -> 1.5 us
    transpose x0 -> x1, local copies, waits for them, and re-layouts: none -> 2.84 us  [shards(): jnp.transpose(cells.reshape(cells.shape[0], -1, TILE), (1, 0, 2))]
where the time goes in v6:
time: 139 us; the launch traced here: 138 us
  Pallas kernels  127 us (91%)
  local copies, waits for them, and re-layouts  5.47 us (4%)
  other arithmetic  5.22 us (4%)
    pallas_call x1, Pallas kernels, transport(): pl.pallas_call(functools.partial(kernel, (n_src, n_tgt, slots)), out_shap...  127 us
    transpose x1, local copies, waits for them, and re-layouts, shards(): jnp.transpose(cells.reshape(cells.shape[0], -1, TILE), (1, 0, 2))  2.84 us

profile of v6, /device:TPU:24, one launch (start us, length us, event | category | flops | bytes accessed | tf_op | source)
XLA Modules:
  0.0 138.2 jit_solution(12772805747443049493)
XLA Ops:
  0.6 1.3 convert_reduce_fusion.1
  2.0 0.6 iota_compare_fusion.5
  2.6 0.8 copy.15
  3.4 0.1 reshape.142
  3.5 0.1 reshape.140
  3.6 0.3 reduce-window.9
  3.9 0.1 slice.19
  4.0 0.1 slice_reduce_fusion
  4.1 0.1 add_bitcast_fusion
  4.2 0.2 select_reduce_fusion
  4.4 0.1 compare_convert_fusion.1
  4.5 0.2 convert_reduce_fusion
  4.7 0.7 iota_select_fusion
  5.4 0.1 select_reduce_fusion.3
  5.5 0.1 compare_convert_fusion
  5.5 0.2 select_reduce_fusion.2
  5.7 0.8 concatenate.3.table
  6.5 0.0 copy-start
  6.5 0.0 copy-start.1
  6.5 2.8 %bitcast_bitcast_fusion = (bf16[128,32,256]{2,1,0:T(8,128)(2,1)S(1)}, bf16[128,32,256]{2,1,0:T(8,128)(2,1)S(1)}) fusion(bf16[4,128,8,256]{3,2,1,0:T(8,128)(2,1)} %bitcast.20, bf16[4,128,8,256]{3,2,1,0:T(8,128)(2,1)} %bitcast.21), kind=kLoop, calls=%fused_computation | loop fusion | bytes 8388608 | tf_op jit(solution)/shard_map/transpose | solution.py:501
  9.3 0.0 copy-done
  9.3 0.0 copy-done.1
  9.3 126.8 %transport.1 = (f32[256,128]{1,0:T(8,128)S(1)}, f32[256,128]{1,0:T(8,128)S(1)}, f32[256,128]{1,0:T(8,128)S(1)}, f32[256,128]{1,0:T(8,128)S(1)}, f32[32,2048]{1,0:T(8,128)S(1)}) custom-call(s32[1280]{0:T(1024)S(1)} %concatenate.3.table, bf16[128,32,256]{2,1,0:T(8,128)(2,1)S(1)} %get-tuple-element.21.xs, bf16[128,32,256]{2,1,0:T(8,128)(2,1)S(1)} %get-tuple-element.20.ys, ...), custom_call_target="tpu_custom_call" | custom-call | tf_op jit(solution)/shard_map/transport/pallas_call | solution.py:454
  136.1 0.7 select_bitcast_fusion.1
  136.8 0.7 select_bitcast_fusion
  137.5 0.7 copy.24
  (6 shorter events, 0.1 us)
Async XLA Ops:
  6.5 2.9 %copy-start = (f32[32768]{0:T(1024)S(1)}, f32[32768]{0:T(1024)}, u32[]{:S(2)}) copy-start(f32[32768]{0:T(1024)} %param.9) | copy-start | bytes 393220
  6.5 2.9 %copy-start.1 = (f32[32768]{0:T(1024)S(1)}, f32[32768]{0:T(1024)}, u32[]{:S(2)}) copy-start(f32[32768]{0:T(1024)} %param.10) | copy-start | bytes 393220

commit v7 on v6

--- a/solution.py
+++ b/solution.py
@@ -72,7 +72,7 @@
     first_y, ring_a, ring_b, last_y, kept, local, *sems,
 ):
     n_src, n_tgt, slots = sizes
-    step = math.gcd(slots, 16)
+    step = math.gcd(slots, 32)
     clusters, features = xs.shape[:2]
     me_src, me_tgt = lax.axis_index("src"), lax.axis_index("tgt")
     barrier = pltpu.get_barrier_semaphore()
@@ -241,8 +241,10 @@
             rows.append(jnp.where(lane < entry(TGT_COUNT, c), -2.0 * squared_norm(ys[c]), EMPTY))
         v0[pl.ds(pl.multiple_of(g * SUB, SUB), SUB), :] = jnp.concatenate(rows, axis=0)
 
-    def norms():
-        @pl.loop(0, clusters // SUB)
+    def norms(part):
+        groups = clusters // SUB // 2
+
+        @pl.loop(part * groups, part * groups + groups)
         def _(g):
             for r in range(SUB):
                 c = g * SUB + r
@@ -259,9 +261,9 @@
                 put_halves(u_out, g * SUB + r, cluster_row(u2, g * SUB + r))
 
     sweep("max", ROW_SUB, ys, xs, v0, u0)
-    reduce("max", 0, "tgt", me_tgt, n_tgt, ROW_LAST, u0, u1, nothing)
+    reduce("max", 0, "tgt", me_tgt, n_tgt, ROW_LAST, u0, u1, lambda: norms(0))
     sweep("max", COL_SUB, xs, ys, u1, v0)
-    reduce("max", 1, "src", me_src, n_src, COL_LAST, v0, v1, norms)
+    reduce("max", 1, "src", me_src, n_src, COL_LAST, v0, v1, lambda: norms(1))
     sweep("sum", ROW_SUB, ys, xs, v1, u1)
     reduce("sum", 2, "tgt", me_tgt, n_tgt, ROW_LAST, u1, u2, nothing)
     sweep("sum", COL_SUB, xs, ys, u2, v1)

time: 139 us -> 135 us (0.971)
  Pallas kernels: 127 us -> 123 us
    pallas_call x1, Pallas kernels: 127 us -> 123 us  [transport(): pl.pallas_call(functools.partial(kernel, (n_src, n_tgt, slots)), out_shap...]
where the time goes in v7:
time: 135 us
  Pallas kernels  123 us (91%)
  local copies, waits for them, and re-layouts  5.47 us (4%)
  other arithmetic  5.22 us (4%)
    pallas_call x1, Pallas kernels, transport(): pl.pallas_call(functools.partial(kernel, (n_src, n_tgt, slots)), out_shap...  123 us
    transpose x1, local copies, waits for them, and re-layouts, shards(): jnp.transpose(cells.reshape(cells.shape[0], -1, TILE), (1, 0, 2))  2.84 us

profile of v7, /device:TPU:24, one launch (start us, length us, event | category | flops | bytes accessed | tf_op | source)
XLA Modules:
  0.0 134.8 jit_solution(8862193404308046795)
XLA Ops:
  0.6 1.3 convert_reduce_fusion.1
  2.0 0.6 iota_compare_fusion.5
  2.6 0.8 copy.15
  3.4 0.1 reshape.142
  3.5 0.1 reshape.140
  3.6 0.3 reduce-window.9
  3.9 0.1 slice.19
  4.0 0.1 slice_reduce_fusion
  4.1 0.1 add_bitcast_fusion
  4.2 0.2 select_reduce_fusion
  4.4 0.1 compare_convert_fusion.1
  4.5 0.2 convert_reduce_fusion
  4.7 0.7 iota_select_fusion
  5.4 0.1 select_reduce_fusion.3
  5.5 0.1 compare_convert_fusion
  5.5 0.2 select_reduce_fusion.2
  5.7 0.8 concatenate.3.table
  6.5 0.0 copy-start
  6.5 0.0 copy-start.1
  6.5 2.8 %bitcast_bitcast_fusion = (bf16[128,32,256]{2,1,0:T(8,128)(2,1)S(1)}, bf16[128,32,256]{2,1,0:T(8,128)(2,1)S(1)}) fusion(bf16[4,128,8,256]{3,2,1,0:T(8,128)(2,1)} %bitcast.20, bf16[4,128,8,256]{3,2,1,0:T(8,128)(2,1)} %bitcast.21), kind=kLoop, calls=%fused_computation | loop fusion | bytes 8388608 | tf_op jit(solution)/shard_map/transpose | solution.py:503
  9.3 0.0 copy-done
  9.3 0.0 copy-done.1
  9.3 123.4 %transport.1 = (f32[256,128]{1,0:T(8,128)S(1)}, f32[256,128]{1,0:T(8,128)S(1)}, f32[256,128]{1,0:T(8,128)S(1)}, f32[256,128]{1,0:T(8,128)S(1)}, f32[32,2048]{1,0:T(8,128)S(1)}) custom-call(s32[1280]{0:T(1024)S(1)} %concatenate.3.table, bf16[128,32,256]{2,1,0:T(8,128)(2,1)S(1)} %get-tuple-element.21.xs, bf16[128,32,256]{2,1,0:T(8,128)(2,1)S(1)} %get-tuple-element.20.ys, ...), custom_call_target="tpu_custom_call" | custom-call | tf_op jit(solution)/shard_map/transport/pallas_call | solution.py:456
  132.8 0.7 select_bitcast_fusion.1
  133.5 0.7 select_bitcast_fusion
  134.1 0.7 copy.24
  (6 shorter events, 0.1 us)
Async XLA Ops:
  6.5 2.9 %copy-start = (f32[32768]{0:T(1024)S(1)}, f32[32768]{0:T(1024)}, u32[]{:S(2)}) copy-start(f32[32768]{0:T(1024)} %param.9) | copy-start | bytes 393220
  6.5 2.9 %copy-start.1 = (f32[32768]{0:T(1024)S(1)}, f32[32768]{0:T(1024)}, u32[]{:S(2)}) copy-start(f32[32768]{0:T(1024)} %param.10) | copy-start | bytes 393220

commit v8 on v7

--- a/solution.py
+++ b/solution.py
@@ -50,10 +50,10 @@
 
 def far_offset(axis, j, n):
     if axis == "tgt":
-        return n // 2 + lax.div(j + 1, 2) * (1 - 2 * lax.rem(j, 2))
-    i = lax.div(j, 2)
-    near = n // 4 + lax.div(i + 1, 2) * (2 * lax.rem(i, 2) - 1)
-    return near + lax.rem(j, 2) * (n - 2 * near)
+        return n // 2 + (j + 1) // 2 * (1 - 2 * (j % 2))
+    i = j // 2
+    near = n // 4 + (i + 1) // 2 * (2 * (i % 2) - 1)
+    return n - near if j % 2 else near
 
 
 def aux_rows(row, offset, other):
@@ -181,10 +181,11 @@
         if which == 0:
             pl.semaphore_wait(barrier, n_src + n_tgt - 2)
 
-        @pl.loop(0, n - 1)
-        def _(j):
+        made = []
+        for j in range(n - 1):
             finish(lax.rem(me + far_offset(axis, j, n), n))
-            copy(j, 0).start()
+            made.append(copy(j, 0))
+            made[-1].start()
 
         finish(me)
         meanwhile()
@@ -197,9 +198,8 @@
             rows.append(jnp.where(lanes < entry(count, me * per + r), jnp.log(halves_row(mass, r)), EMPTY))
         logmass = jnp.concatenate(rows, axis=0)
 
-        @pl.loop(0, n - 1)
-        def _(j):
-            copy(j, 0).wait_recv()
+        for each in made:
+            each.wait_recv()
 
         mine = shard(me)
         own = part[mine, :]
@@ -218,17 +218,13 @@
             lse = jnp.log(jnp.where(total > 0.0, total, 1.0))
         new[mine, :] = jnp.where(logmass > 0.5 * EMPTY, old[mine, :] + logmass - lse, EMPTY)
 
-        @pl.loop(0, n - 1)
-        def _(j):
-            copy(j, 1).start()
-
-        @pl.loop(0, n - 1)
-        def _(j):
-            copy(j, 0).wait_send()
-
-        @pl.loop(0, n - 1)
-        def _(j):
-            copy(j, 1).wait()
+        sent = [copy(j, 1) for j in range(n - 1)]
+        for each in sent:
+            each.start()
+        for each in made:
+            each.wait_send()
+        for each in sent:
+            each.wait()
 
     lane = lax.broadcasted_iota(jnp.int32, (1, TILE), 1)
     u0[...] = jnp.zeros(u0.shape, jnp.float32)
@@ -465,32 +461,35 @@
 
 
 def pair_tables(pair_lists, tgt_block, per_block, slots, counts):
-    width = pair_lists.shape[1]
-    flat = pair_lists.reshape(-1)
-    chosen = flat // per_block == tgt_block
-    targets = flat % per_block
-    sources = jnp.arange(flat.shape[0], dtype=jnp.int32) // width
+    lists = pair_lists.T
+    chosen = lists // per_block == tgt_block
+    targets = lists % per_block
+    sources = lax.broadcasted_iota(jnp.int32, lists.shape, 1)
     places = jnp.arange(slots, dtype=jnp.int32)
-    rank = jnp.cumsum(chosen.astype(jnp.int32)) - 1
-    matches = (rank[None, :] == places[:, None]) & chosen[None, :]
-    row_src = jnp.sum(jnp.where(matches, sources[None, :], 0), axis=1)
-    row_tgt = jnp.sum(jnp.where(matches, targets[None, :], 0), axis=1)
-    live = places < jnp.sum(chosen.astype(jnp.int32))
+
+    def counted(which):
+        upto = jnp.sum((chosen[None] & (which[None] <= places[:, None, None])).astype(jnp.int32), axis=(1, 2))
+        equal = jnp.sum((chosen[None] & (which[None] == places[:, None, None])).astype(jnp.int32), axis=(1, 2))
+        return upto, equal
+
+    def kept(upto, equal):
+        cluster = jnp.sum((upto[None, :] <= places[:, None]).astype(jnp.int32), axis=1)
+        before = jnp.sum((upto[None, :] < places[:, None]).astype(jnp.int32), axis=1)
+        cluster = jnp.minimum(cluster, per_block - 1)
+        return cluster, (cluster == before).astype(jnp.int32), jnp.where(equal > 0, upto - 1, slots)
+
+    upto, equal = counted(sources)
+    row_src, row_keep, row_last = kept(upto, equal)
+    col_upto, col_equal = counted(targets)
+    col_tgt, col_keep, col_last = kept(col_upto, col_equal)
+    within = jnp.cumsum(chosen.astype(jnp.int32), axis=0)
+    rank = jnp.where(chosen, (upto - equal)[None, :] + within - 1, -1)
+    row_tgt = jnp.sum(jnp.where(rank[None] == places[:, None, None], targets[None], 0), axis=(1, 2))
+    live = places < upto[-1]
     before = (row_tgt[None, :] < row_tgt[:, None]) | (
         (row_tgt[None, :] == row_tgt[:, None]) & (places[None, :] < places[:, None]))
-    order = jnp.where(live, jnp.sum((before & live[None, :]).astype(jnp.int32), axis=1), places)
-    moves = order[None, :] == places[:, None]
-    col_src = jnp.sum(jnp.where(moves, row_src[None, :], 0), axis=1)
-    col_tgt = jnp.sum(jnp.where(moves, row_tgt[None, :], 0), axis=1)
-
-    def ends(kept):
-        same = jnp.concatenate([jnp.zeros((1,), jnp.int32), (kept[1:] == kept[:-1]).astype(jnp.int32)])
-        found = (kept[None, :] == places[:, None]) & live[None, :]
-        last = jnp.max(jnp.where(found, places[None, :], -1), axis=1)
-        return same, jnp.where(last < 0, slots, last)
-
-    row_keep, row_last = ends(row_src)
-    col_keep, col_last = ends(col_tgt)
+    order = jnp.where(live, jnp.sum((before & live[None, :]).astype(jnp.int32), axis=1), -1)
+    col_src = jnp.sum(jnp.where(order[None, :] == places[:, None], row_src[None, :], 0), axis=1)
     return jnp.concatenate([row_tgt, row_src, row_keep, row_last, col_src, col_tgt, col_keep, col_last] + counts)
 
 

time: 135 us -> 146 us (1.081)
  other arithmetic: 5.22 us -> 16 us
    reduce_sum x4 -> x5, other arithmetic: 1.83 us -> 11.9 us  [the longest x2 11.5 us: counted(): jnp.sum((chosen[None] & (which[None] == places[:, None, None])).astype(jn...]
where the time goes in v8:
time: 146 us
  Pallas kernels  123 us (84%)
  other arithmetic  16 us (11%)
  local copies, waits for them, and re-layouts  5.48 us (4%)
    pallas_call x1, Pallas kernels, transport(): pl.pallas_call(functools.partial(kernel, (n_src, n_tgt, slots)), out_shap...  123 us
    reduce_sum x2, other arithmetic, counted(): jnp.sum((chosen[None] & (which[None] == places[:, None, None])).astype(jn...  11.5 us

profile of v8, /device:TPU:24, one launch (start us, length us, event | category | flops | bytes accessed | tf_op | source)
XLA Modules:
  0.0 145.6 jit_solution(3682271817626516362)
XLA Ops:
  0.6 0.7 add_select_fusion
  1.3 0.7 fusion.11
  2.1 4.6 %convert_reduce_fusion.2 = (s32[128]{0:T(128)S(1)}, s32[128]{0:T(128)S(1)}) fusion(pred[8,128]{1,0:T(8,128)(4,1)S(1)} %get-tuple-element.23), kind=kLoop, calls=%fused_computation.8 | loop fusion | flops 1048320 | bytes 2048 | tf_op jit(solution)/shard_map/reduce_sum | solution.py:472
  6.7 0.6 slice.3
  7.3 6.9 %convert_reduce_fusion = (s32[128]{0:T(128)S(1)}, s32[128]{0:T(128)S(1)}, s32[128]{0:T(128)S(1)}) fusion(s32[8,128]{1,0:T(8,128)S(1)} %add_select_fusion, pred[8,128]{1,0:T(8,128)(4,1)S(1)} %get-tuple-element.23, s32[8,128]{1,0:T(8,128)S(1)} %add_select_fusion.2), kind=kLoop, calls=%fused_computation.2 | loop fusion | flops 1441408 | bytes 10752 | tf_op jit(solution)/shard_map/reduce_sum | solution.py:472
  14.2 0.7 iota_compare_fusion.11
  14.8 0.2 convert_reduce_fusion.4
  15.0 0.7 broadcast_select_fusion
  15.7 0.1 convert_reduce_fusion.7
  15.8 0.1 select_reduce_fusion.1
  16.0 0.7 constant_dynamic-update-slice_fusion.1
  16.7 0.7 constant_dynamic-update-slice_fusion.table
  17.3 0.0 copy-start
  17.3 0.0 copy-start.1
  17.3 2.8 %bitcast_bitcast_fusion = (bf16[128,32,256]{2,1,0:T(8,128)(2,1)S(1)}, bf16[128,32,256]{2,1,0:T(8,128)(2,1)S(1)}) fusion(bf16[4,128,8,256]{3,2,1,0:T(8,128)(2,1)} %bitcast.46, bf16[4,128,8,256]{3,2,1,0:T(8,128)(2,1)} %bitcast.47), kind=kLoop, calls=%fused_computation | loop fusion | bytes 8388608 | tf_op jit(solution)/shard_map/transpose | solution.py:502
  20.2 0.0 copy-done
  20.2 0.0 copy-done.1
  20.2 123.3 %transport.1 = (f32[256,128]{1,0:T(8,128)S(1)}, f32[256,128]{1,0:T(8,128)S(1)}, f32[256,128]{1,0:T(8,128)S(1)}, f32[256,128]{1,0:T(8,128)S(1)}, f32[32,2048]{1,0:T(8,128)S(1)}) custom-call(s32[1280]{0:T(1024)S(1)} %constant_dynamic-update-slice_fusion.table, bf16[128,32,256]{2,1,0:T(8,128)(2,1)S(1)} %get-tuple-element.28.xs, ...), custom_call_target="tpu_custom_call" | custom-call | tf_op jit(solution)/shard_map/transport/pallas_call | solution.py:452
  143.5 0.7 select_bitcast_fusion.1
  144.2 0.7 select_bitcast_fusion
  144.9 0.7 copy.29
  (12 shorter events, 0.1 us)
Async XLA Ops:
  17.3 2.9 %copy-start = (f32[32768]{0:T(1024)S(1)}, f32[32768]{0:T(1024)}, u32[]{:S(2)}) copy-start(f32[32768]{0:T(1024)} %param.9) | copy-start | bytes 393220
  17.3 2.9 %copy-start.1 = (f32[32768]{0:T(1024)S(1)}, f32[32768]{0:T(1024)}, u32[]{:S(2)}) copy-start(f32[32768]{0:T(1024)} %param.10) | copy-start | bytes 393220

commit v9 on v7

--- a/solution.py
+++ b/solution.py
@@ -68,7 +68,7 @@
 
 def kernel(
     sizes, table, xs, ys, x_mass, y_mass, u_out, v_out, x_norm_out, y_norm_out, out,
-    masses, u0, v0, u1, v1, u2, v2, parts, helds, slot_m, slot_s, slot_n, slot_d, send_a, send_y, den, held_d,
+    masses, u0, v0, u1, v1, u2, v2, parts, helds, slot_m, slot_s, slot_n, slot_d, send_a, send_y,
     first_y, ring_a, ring_b, last_y, kept, local, *sems,
 ):
     n_src, n_tgt, slots = sizes
@@ -288,7 +288,11 @@
         return lax.rem(z + sign[d] * (hops[g][d] - hop) + nz, nz)
 
     def own(at, side, g, c):
-        return slot_n[entry(ROW_LAST, (at * NY + side) * per + g * half + c)]
+        slot = entry(ROW_LAST, (at * NY + side) * per + g * half + c)
+        return slot_n[slot], slot_d[pl.ds(slot, 1), :]
+
+    def plus(*terms):
+        return tuple(functools.reduce(jnp.add, term) for term in zip(*terms))
 
     def copy(src, dst, sem, k, peer):
         made = pltpu.make_async_remote_copy(
@@ -297,24 +301,36 @@
         made.start()
         return made
 
+    def exponent_of(value):
+        return jnp.ceil(jnp.log2(jnp.maximum(value, 1e-30)))
+
+    def coded(value, exponent):
+        return jnp.floor(value * (jnp.exp2(-exponent) * CODE) + 0.5)
+
     def encode(ref, values):
-        exponents = []
+        rows = [[], [], []]
         for c in range(half):
-            value = values(c)
-            largest = jnp.max(jnp.abs(value), axis=0, keepdims=True)
-            exponent = jnp.ceil(jnp.log2(jnp.maximum(largest, 1e-30)))
-            code = jnp.floor(value * (jnp.exp2(-exponent) * CODE) + 0.5)
+            value, weight = values(c)
+            exponent = exponent_of(jnp.max(jnp.abs(value), axis=0, keepdims=True))
+            code = coded(value, exponent)
             ref[c * features:(c + 1) * features, :] = code.astype(jnp.int32).astype(jnp.int16)
-            exponents.append(exponent)
-        exponents.append(jnp.zeros((AUX - half, TILE), jnp.float32))
-        block = jnp.concatenate(exponents, axis=0)
+            at = exponent_of(weight)
+            for row, item in zip(rows, (exponent, at, coded(weight, at))):
+                row.append(item)
+        spare = [jnp.zeros((AUX - 3 * half, TILE), jnp.float32)]
+        block = jnp.concatenate(rows[0] + rows[1] + rows[2] + spare, axis=0)
         ref[half * features:half * features + AUX, :] = block.astype(jnp.int32).astype(jnp.int16)
 
     def decoder(ref):
-        exponents = ref[half * features:half * features + AUX, :].astype(jnp.int32).astype(jnp.float32)
-        scale = jnp.exp2(exponents) * (1.0 / CODE)
-        return lambda c: (
-            ref[c * features:(c + 1) * features, :].astype(jnp.int32).astype(jnp.float32) * scale[c:c + 1])
+        block = ref[half * features:half * features + AUX, :].astype(jnp.int32).astype(jnp.float32)
+        scale = jnp.exp2(block[:2 * half]) * (1.0 / CODE)
+
+        def decode(c):
+            code = ref[c * features:(c + 1) * features, :].astype(jnp.int32).astype(jnp.float32)
+            weight = block[2 * half + c:2 * half + c + 1] * scale[half + c:half + c + 1]
+            return code * scale[c:c + 1], weight
+
+        return decode
 
     pieces = [(d, hop) for hop in range(far) for d in range(2) if hop < hops[1][d]]
     over_y = {}
@@ -336,16 +352,6 @@
         send_piece(i, block(1, d, hop))
     send_piece(nz - 1, z)
 
-    def gather(t):
-        for c in range(per):
-            den[t, pl.ds(c, 1), :] = slot_d[pl.ds(entry(ROW_LAST, t * per + c), 1), :]
-
-    pl.loop(0, n)(gather)
-    others = []
-    for k in range(1, n):
-        peer = lax.rem(me_tgt + k, n)
-        others.append(copy(den.at[peer], held_d.at[k], 6, k, peer))
-
     def step_b(d, hop):
         i = pieces.index((d, hop))
         over_y[i].wait_recv()
@@ -354,7 +360,7 @@
             over_b[d, hop - 1].wait_recv()
             parts_of.append(decoder(ring_b.at[d, hop - 1]))
         at = block(1, d, hop)
-        encode(first_y.at[i], lambda c: sum((part(c) for part in parts_of), own(at, y, 1, c)))
+        encode(first_y.at[i], lambda c: plus(own(at, y, 1, c), *(part(c) for part in parts_of)))
         over_b[d, hop] = copy(first_y.at[i], ring_b.at[d, hop], 4, d * far + hop, toward(d))
 
     def step_a(d, s, hop):
@@ -362,7 +368,7 @@
         held = ring_a.at[d, hop - 1, s]
         arrived = decoder(held)
         at = block(0, d, hop)
-        encode(held, lambda c: arrived(c) + own(at, sides[s], 0, c))
+        encode(held, lambda c: plus(arrived(c), own(at, sides[s], 0, c)))
         over_a[d, s, hop] = copy(held, ring_a.at[d, hop, s], 3, (d * NY + s) * far + hop, toward(d))
 
     for hop in range(far):
@@ -379,7 +385,7 @@
         for d in range(2):
             over_a[d, s, hops[0][d] - 1].wait_recv()
             both.append(decoder(ring_a.at[d, hops[0][d] - 1, s]))
-        return lambda c: both[0](c) + both[1](c) + own(z, sides[s], 0, c)
+        return lambda c: plus(both[0](c), both[1](c), own(z, sides[s], 0, c))
 
     encode(kept, arrived_a(0))
     over_last = copy(kept, last_y, 5, 0, partner)
@@ -389,15 +395,9 @@
         for r in range(SUB):
             put_halves(v_out, g * SUB + r, cluster_row(v2, g * SUB + r))
 
-    for made in others:
-        made.wait_recv()
-    total = den[me_tgt]
-    for k in range(1, n):
-        total = total + held_d[k]
-    total = jnp.where(total > 0.0, total, 1.0)
-
-    def put(c, value):
-        out[:, c * TILE:(c + 1) * TILE] = value / total[c:c + 1]
+    def put(c, sums):
+        value, weight = sums
+        out[:, c * TILE:(c + 1) * TILE] = value / jnp.where(weight > 0.0, weight, 1.0)
 
     over_y[nz - 1].wait_recv()
     parts_b = [decoder(first_y.at[nz - 1])]
@@ -405,13 +405,13 @@
         over_b[d, hops[1][d] - 1].wait_recv()
         parts_b.append(decoder(ring_b.at[d, hops[1][d] - 1]))
     for c in range(half):
-        put(half + c, sum((part(c) for part in parts_b), own(z, y, 1, c)))
+        put(half + c, plus(own(z, y, 1, c), *(part(c) for part in parts_b)))
     mine = arrived_a(1)
     over_last.wait_recv()
     last = decoder(last_y)
     for c in range(half):
-        put(c, mine(c) + last(c))
-    for made in others + [over_last] + list(over_y.values()) + list(over_a.values()) + list(over_b.values()):
+        put(c, plus(mine(c), last(c)))
+    for made in [over_last] + list(over_y.values()) + list(over_a.values()) + list(over_b.values()):
         made.wait_send()
 
 
@@ -426,7 +426,7 @@
     dma = pltpu.SemaphoreType.DMA
     most = max(n_src, n_tgt)
     sems = [dma((4, most))] * 4
-    for many in (nz, 2 * NY * far, 2 * far, 1, n_tgt):
+    for many in (nz, 2 * NY * far, 2 * far, 1):
         sems += [dma((many,))] * 2
     flat = jax.ShapeDtypeStruct((2 * clusters, TILE // 2), f32)
     row = pltpu.VMEM((clusters, TILE), f32)
@@ -444,8 +444,6 @@
         pltpu.VMEM((slots + SUB, TILE), f32),
         codes(2, NY),
         codes(nz),
-        pltpu.VMEM((n_tgt, per, TILE), f32),
-        pltpu.VMEM((n_tgt, per, TILE), f32),
         codes(nz),
         codes(2, far, NY),
         codes(2, far),
@@ -475,7 +473,7 @@
     matches = (rank[None, :] == places[:, None]) & chosen[None, :]
     row_src = jnp.sum(jnp.where(matches, sources[None, :], 0), axis=1)
     row_tgt = jnp.sum(jnp.where(matches, targets[None, :], 0), axis=1)
-    live = places < jnp.sum(chosen.astype(jnp.int32))
+    live = jnp.sum(matches.astype(jnp.int32), axis=1) > 0
     before = (row_tgt[None, :] < row_tgt[:, None]) | (
         (row_tgt[None, :] == row_tgt[:, None]) & (places[None, :] < places[:, None]))
     order = jnp.where(live, jnp.sum((before & live[None, :]).astype(jnp.int32), axis=1), places)

time: 135 us -> 131 us (0.970)
  other arithmetic: 5.22 us -> 2.65 us
    pallas_call x1, Pallas kernels: 123 us -> 122 us  [transport(): pl.pallas_call(functools.partial(kernel, (n_src, n_tgt, slots)), out_shap...]
where the time goes in v9:
time: 131 us
  Pallas kernels  122 us (93%)
  local copies, waits for them, and re-layouts  5.47 us (4%)
  other arithmetic  2.65 us (2%)
    pallas_call x1, Pallas kernels, transport(): pl.pallas_call(functools.partial(kernel, (n_src, n_tgt, slots)), out_shap...  122 us
    transpose x1, local copies, waits for them, and re-layouts, shards(): jnp.transpose(cells.reshape(cells.shape[0], -1, TILE), (1, 0, 2))  2.84 us

profile of v9, /device:TPU:24, one launch (start us, length us, event | category | flops | bytes accessed | tf_op | source)
XLA Modules:
  0.0 130.9 jit_solution(17134360147144809714)
XLA Ops:
  0.6 0.8 copy.15
  1.4 0.1 reshape.142
  1.5 0.1 reshape.140
  1.6 0.3 reduce-window.9
  1.9 0.1 slice.19
  2.0 0.1 slice_reduce_fusion
  2.1 0.1 add_bitcast_fusion
  2.2 0.3 convert_reduce_fusion
  2.5 0.2 convert_reduce_fusion.1
  2.7 0.1 select_reduce_fusion.3
  2.8 0.1 compare_convert_fusion
  2.9 0.1 compare_convert_fusion.1
  3.0 0.2 select_reduce_fusion.2
  3.1 0.8 concatenate.3.table
  3.9 0.0 copy-start
  3.9 0.0 copy-start.1
  3.9 2.8 %bitcast_bitcast_fusion = (bf16[128,32,256]{2,1,0:T(8,128)(2,1)S(1)}, bf16[128,32,256]{2,1,0:T(8,128)(2,1)S(1)}) fusion(bf16[4,128,8,256]{3,2,1,0:T(8,128)(2,1)} %bitcast.20, bf16[4,128,8,256]{3,2,1,0:T(8,128)(2,1)} %bitcast.21), kind=kLoop, calls=%fused_computation | loop fusion | bytes 8388608 | tf_op jit(solution)/shard_map/transpose | solution.py:501
  6.7 0.0 copy-done
  6.8 0.0 copy-done.1
  6.8 122.0 %transport.1 = (f32[256,128]{1,0:T(8,128)S(1)}, f32[256,128]{1,0:T(8,128)S(1)}, f32[256,128]{1,0:T(8,128)S(1)}, f32[256,128]{1,0:T(8,128)S(1)}, f32[32,2048]{1,0:T(8,128)S(1)}) custom-call(s32[1280]{0:T(1024)S(1)} %concatenate.3.table, bf16[128,32,256]{2,1,0:T(8,128)(2,1)S(1)} %get-tuple-element.22.xs, bf16[128,32,256]{2,1,0:T(8,128)(2,1)S(1)} %get-tuple-element.21.ys, ...), custom_call_target="tpu_custom_call" | custom-call | tf_op jit(solution)/shard_map/transport/pallas_call | solution.py:454
  128.8 0.7 select_bitcast_fusion.1
  129.5 0.7 select_bitcast_fusion
  130.2 0.7 copy.24
  (8 shorter events, 0.1 us)
Async XLA Ops:
  3.9 2.9 %copy-start = (f32[32768]{0:T(1024)S(1)}, f32[32768]{0:T(1024)}, u32[]{:S(2)}) copy-start(f32[32768]{0:T(1024)} %param.9) | copy-start | bytes 393220
  3.9 2.9 %copy-start.1 = (f32[32768]{0:T(1024)S(1)}, f32[32768]{0:T(1024)}, u32[]{:S(2)}) copy-start(f32[32768]{0:T(1024)} %param.10) | copy-start | bytes 393220

commit v10 on v9

--- a/solution.py
+++ b/solution.py
@@ -72,7 +72,7 @@
     first_y, ring_a, ring_b, last_y, kept, local, *sems,
 ):
     n_src, n_tgt, slots = sizes
-    step = math.gcd(slots, 32)
+    step = math.gcd(slots, 64)
     clusters, features = xs.shape[:2]
     me_src, me_tgt = lax.axis_index("src"), lax.axis_index("tgt")
     barrier = pltpu.get_barrier_semaphore()
@@ -341,15 +341,18 @@
         encode(send_y.at[i], lambda c: own(at, other, 1, c))
         over_y[i] = copy(send_y.at[i], first_y.at[i], 2, i, partner)
 
+    def start_a(d, s):
+        encode(send_a.at[d, s], lambda c: own(block(0, d, 0), sides[s], 0, c))
+        over_a[d, s, 0] = copy(send_a.at[d, s], ring_a.at[d, 0, s], 3, (d * NY + s) * far, toward(d))
+
+    for d in range(2):
+        start_a(d, 0)
     for i in range(2):
-        d, hop = pieces[i]
-        send_piece(i, block(1, d, hop))
-        for s in range(NY):
-            encode(send_a.at[i, s], lambda c: own(block(0, i, 0), sides[s], 0, c))
-            over_a[i, s, 0] = copy(send_a.at[i, s], ring_a.at[i, 0, s], 3, (i * NY + s) * far, toward(i))
+        send_piece(i, block(1, *pieces[i]))
+    for d in range(2):
+        start_a(d, 1)
     for i in range(2, nz - 1):
-        d, hop = pieces[i]
-        send_piece(i, block(1, d, hop))
+        send_piece(i, block(1, *pieces[i]))
     send_piece(nz - 1, z)
 
     def step_b(d, hop):
@@ -371,15 +374,6 @@
         encode(held, lambda c: plus(arrived(c), own(at, sides[s], 0, c)))
         over_a[d, s, hop] = copy(held, ring_a.at[d, hop, s], 3, (d * NY + s) * far + hop, toward(d))
 
-    for hop in range(far):
-        for d in range(2):
-            if hop < hops[1][d]:
-                step_b(d, hop)
-        for s in range(NY):
-            for d in range(2):
-                if 0 < hop < hops[0][d]:
-                    step_a(d, s, hop)
-
     def arrived_a(s):
         both = []
         for d in range(2):
@@ -387,8 +381,19 @@
             both.append(decoder(ring_a.at[d, hops[0][d] - 1, s]))
         return lambda c: plus(both[0](c), both[1](c), own(z, sides[s], 0, c))
 
-    encode(kept, arrived_a(0))
-    over_last = copy(kept, last_y, 5, 0, partner)
+    for hop in range(1, far + 1):
+        for d in range(2):
+            if hop < hops[0][d]:
+                step_a(d, 0, hop)
+        if hop == far:
+            encode(kept, arrived_a(0))
+            over_last = copy(kept, last_y, 5, 0, partner)
+        for d in range(2):
+            if hop - 1 < hops[1][d]:
+                step_b(d, hop - 1)
+        for d in range(2):
+            if hop < hops[0][d]:
+                step_a(d, 1, hop)
 
     @pl.loop(0, clusters // SUB)
     def _(g):

time: 131 us -> 126 us (0.962)
  Pallas kernels: 122 us -> 117 us
    pallas_call x1, Pallas kernels: 122 us -> 117 us  [transport(): pl.pallas_call(functools.partial(kernel, (n_src, n_tgt, slots)), out_shap...]
where the time goes in v10:
time: 126 us
  Pallas kernels  117 us (93%)
  local copies, waits for them, and re-layouts  5.47 us (4%)
  other arithmetic  2.65 us (2%)
    pallas_call x1, Pallas kernels, transport(): pl.pallas_call(functools.partial(kernel, (n_src, n_tgt, slots)), out_shap...  117 us
    transpose x1, local copies, waits for them, and re-layouts, shards(): jnp.transpose(cells.reshape(cells.shape[0], -1, TILE), (1, 0, 2))  2.84 us

profile of v10, /device:TPU:24, one launch (start us, length us, event | category | flops | bytes accessed | tf_op | source)
XLA Modules:
  0.0 125.6 jit_solution(15955801511546871016)
XLA Ops:
  0.6 0.8 copy.15
  1.4 0.1 reshape.142
  1.5 0.1 reshape.140
  1.6 0.3 reduce-window.9
  1.9 0.1 slice.19
  2.0 0.1 slice_reduce_fusion
  2.1 0.1 add_bitcast_fusion
  2.2 0.3 convert_reduce_fusion
  2.5 0.2 convert_reduce_fusion.1
  2.7 0.1 select_reduce_fusion.3
  2.8 0.1 compare_convert_fusion
  2.9 0.1 compare_convert_fusion.1
  3.0 0.2 select_reduce_fusion.2
  3.1 0.8 concatenate.3.table
  3.9 0.0 copy-start
  3.9 0.0 copy-start.1
  3.9 2.8 %bitcast_bitcast_fusion = (bf16[128,32,256]{2,1,0:T(8,128)(2,1)S(1)}, bf16[128,32,256]{2,1,0:T(8,128)(2,1)S(1)}) fusion(bf16[4,128,8,256]{3,2,1,0:T(8,128)(2,1)} %bitcast.20, bf16[4,128,8,256]{3,2,1,0:T(8,128)(2,1)} %bitcast.21), kind=kLoop, calls=%fused_computation | loop fusion | bytes 8388608 | tf_op jit(solution)/shard_map/transpose | solution.py:506
  6.7 0.0 copy-done
  6.8 0.0 copy-done.1
  6.8 116.7 %transport.1 = (f32[256,128]{1,0:T(8,128)S(1)}, f32[256,128]{1,0:T(8,128)S(1)}, f32[256,128]{1,0:T(8,128)S(1)}, f32[256,128]{1,0:T(8,128)S(1)}, f32[32,2048]{1,0:T(8,128)S(1)}) custom-call(s32[1280]{0:T(1024)S(1)} %concatenate.3.table, bf16[128,32,256]{2,1,0:T(8,128)(2,1)S(1)} %get-tuple-element.22.xs, bf16[128,32,256]{2,1,0:T(8,128)(2,1)S(1)} %get-tuple-element.21.ys, ...), custom_call_target="tpu_custom_call" | custom-call | tf_op jit(solution)/shard_map/transport/pallas_call | solution.py:459
  123.5 0.7 select_bitcast_fusion.1
  124.2 0.7 select_bitcast_fusion
  124.9 0.7 copy.24
  (8 shorter events, 0.1 us)
Async XLA Ops:
  3.9 2.9 %copy-start = (f32[32768]{0:T(1024)S(1)}, f32[32768]{0:T(1024)}, u32[]{:S(2)}) copy-start(f32[32768]{0:T(1024)} %param.9) | copy-start | bytes 393220
  3.9 2.9 %copy-start.1 = (f32[32768]{0:T(1024)S(1)}, f32[32768]{0:T(1024)}, u32[]{:S(2)}) copy-start(f32[32768]{0:T(1024)} %param.10) | copy-start | bytes 393220
